TPU v7x, 256 devices: a whole 4x4x8 slice. The times are simulated.
256 devices in a mesh: row: 8 (over y, core), col: 32 (over z, x).
Axes of the slice: x: 4, y: 4, z: 8, core: 2. Of those that a mesh axis runs over, the one named last changes fastest.
Arguments:
- amplitudes: float32 [320, 102400], P('col', 'row'), may hold values from -6 to 6
- integral: float32 [20480, 25600], P('col', 'row'), may hold values from -0.0390625 to 0.0390625
- residual_in: float32 [1280, 20480], P('col', 'row'), may hold values from -6 to 6
Outputs:
- residual_out: float32 [1280, 20480], P('col', 'row')
All inputs are finite; a program needn't handle non-finite values.
Results may differ from a plain program's by a relative error of at most 0.00005.
Values sent between devices are 32-bit elements; how exact they have to be, the bound alone decides.
No kernel may reach another device: no remote copies, remote signals or barrier semaphores. Data moves between devices by JAX's collectives and lax.ppermute only.
A program may use at most 256 MiB of HBM per device.

v0:
```python
import jax
import jax.numpy as jnp
from jax import lax
from jax.sharding import PartitionSpec as P

O = 80
V = 320
NI = 4
NJ = 64


def per_device(amplitudes, integral, residual_in):
    row_count = lax.axis_size("row")
    k_local = O // row_count
    b_local = integral.shape[0] // NJ
    coupling = integral.reshape(b_local * NJ, k_local, V)
    piece = lax.all_gather(amplitudes, "col", axis=0, tiled=True)
    right = piece.reshape(piece.shape[0], k_local, NI * V)
    product = lax.dot_general(
        coupling,
        right,
        (((1, 2), (1, 0)), ((), ())),
        precision=lax.Precision.HIGHEST,
        preferred_element_type=jnp.float32,
    )
    term = product.reshape(b_local, NJ, NI, V).transpose(0, 2, 1, 3).reshape(b_local * NI, NJ * V)
    cycle_block = lax.psum_scatter(term, "row", scatter_dimension=1, tiled=True)
    return residual_in + cycle_block


def solution(mesh):
    return jax.shard_map(
        per_device,
        mesh=mesh,
        in_specs=(P("col", "row"), P("col", "row"), P("col", "row")),
        out_specs=P("col", "row"),
        check_vma=False,
    )
```

profile of v0, /device:TPU:2, one launch (start us, length us, event | category | flops | bytes accessed | tf_op | source)
XLA Modules:
  0.0 388.3 jit_solution(9560752376809360110)
XLA Ops:
  6.5 0.0 all-gather.3.cloned.1.call-start
  6.5 0.7 all-gather.3.cloned.1.call-update
  7.3 0.0 reduce-scatter.2.cloned.1.call-start
  7.3 12.9 %dot_general.9 = f32[10,64,10,320]{3,2,1,0:T(8,128)} reshape(f32[640,3200]{1,0:T(8,128)} %param.4) | data formatting | bytes 16384000 | tf_op jit(solution)/shard_map/dot_general | solution.py:19
  20.2 181.3 %all-gather.3.cloned.1.call-done = f32[32,10,12800]{2,1,0:T(8,128)} async-done(((f32[1,10,12800]{2,1,0:T(8,128)}), f32[32,10,12800]{2,1,0:T(8,128)}) %all-gather.3.cloned.1.call-update) | async-done | bytes 16384016 | tf_op jit(solution)/shard_map/all_gather | solution.py:17
  201.6 24.0 %reshape.11 = f32[320,10,1280]{2,1,0:T(8,128)} reshape(f32[32,10,12800]{2,1,0:T(8,128)} %all-gather.3.cloned.1.call-done) | data formatting | bytes 32768000 | tf_op jit(solution)/shard_map/reshape | solution.py:18
  225.6 26.6 %reshape.19 = f32[4,320,10,320]{1,0,2,3:T(4,128)} reshape(f32[1280,10,320]{0,1,2:T(8,128)} %bitcast.17) | data formatting | bytes 32768000 | tf_op jit(solution)/shard_map/dot_general | solution.py:19
  252.2 26.1 %copy.10 = f32[4,320,10,320]{3,1,2,0:T(8,128)} copy(f32[4,320,10,320]{1,0,2,3:T(4,128)} %reshape.19) | data formatting | bytes 32768000 | tf_op jit(solution)/shard_map/dot_general | solution.py:19
  278.3 0.0 copy-start
  278.3 59.4 %fusion.3 = f32[10,4,64,320]{3,2,1,0:T(8,128)} fusion(f32[4,320,10,320]{3,1,2,0:T(8,128)} %copy.10, f32[10,64,10,320,1]{3,2,1,0,4:T(8,128)} %bitcast.18), kind=kOutput, calls=%fused_computation.3 | convolution fusion | flops 31457280000 | bytes 27852800 | tf_op jit(solution)/shard_map/dot_general | solution.py:19
  337.6 4.9 %reshape.12 = f32[40,20480]{1,0:T(8,128)} reshape(f32[10,4,64,320]{3,2,1,0:T(8,128)} %fusion.3) | data formatting | bytes 6553600 | tf_op jit(solution)/shard_map/reshape | solution.py:26
  342.6 0.0 reduce-scatter.2.cloned.1.call-update
  342.6 37.1 %reduce-scatter.2.cloned.1.call-done = f32[40,2560]{1,0:T(8,128)} async-done(((f32[40,20480]{1,0:T(8,128)}), f32[40,2560]{1,0:T(8,128)}) %reduce-scatter.2.cloned.1.call-update) | async-done | bytes 409616 | tf_op jit(solution)/shard_map/reduce_scatter | solution.py:27
  379.7 0.0 copy-done
  379.7 1.8 add.5
Async XLA Ops:
  6.5 195.0 %all-gather.3.cloned.1.call-start = ((), (), s32[]{:S(2)}) async-start(), calls=%async_computation.2 | async-start | bytes 27033600 | tf_op jit(solution)/shard_map/all_gather | solution.py:17
  7.3 372.4 %reduce-scatter.2.cloned.1.call-start = ((), (), s32[]{:S(2)}) async-start(), calls=%async_computation.1 | async-start | bytes 3686400 | tf_op jit(solution)/shard_map/reduce_scatter | solution.py:27
  278.3 101.4 %copy-start = (f32[40,2560]{1,0:T(8,128)S(1)}, f32[40,2560]{1,0:T(8,128)}, u32[]{:S(2)}) copy-start(f32[40,2560]{1,0:T(8,128)} %param.5) | copy-start | bytes 1228804
Sparse Core Ops, SparseCore 0:
  9.9 191.5 all-gather.2
  342.7 36.9 reduce-scatter.1
where the time goes:
time: 390 us; the launch traced here: 388 us
  waiting for transfers between devices  219 us (56%)
  local copies, waits for them, and re-layouts  94.6 us (24%)
  matrix products  59.4 us (15%)
  between operations  13.4 us (3%)
    all_gather x1, waiting for transfers between devices, per_device(): piece = lax.all_gather(amplitudes, 'col', axis=0, tiled=True)  181 us
    dot_general x3, local copies, waits for them, and re-layouts, per_device(): lax.dot_general(coupling, right, (((1, 2), (1, 0)), ((), ())), precision=...  65.7 us
    dot_general x1, matrix products, per_device(): lax.dot_general(coupling, right, (((1, 2), (1, 0)), ((), ())), precision=...  59.4 us
    reduce_scatter x1, waiting for transfers between devices, per_device(): cycle_block = lax.psum_scatter(term, 'row', scatter_dimension=1, tiled=True)  37.1 us
    reshape x1, local copies, waits for them, and re-layouts, per_device(): right = piece.reshape(piece.shape[0], k_local, NI * V)  24 us
  transfers between devices with their start and end apart: 2, of which 2 were waited for; matrix products, arithmetic and copies ran while one was open for 3% of the time, Pallas kernels for 0%

commit v1 on v0

v1 whole, which is shorter than its diff:
```python
import functools

import jax
import jax.numpy as jnp
from jax import lax
from jax.experimental import pallas as pl
from jax.experimental.pallas import tpu as pltpu
from jax.sharding import PartitionSpec as P

O = 80
V = 320
NI = 4
NJ = 64
LANES = 128
TILES = 2


def split(x):
    high = x.astype(jnp.bfloat16)
    return high, (x - high.astype(jnp.float32)).astype(jnp.bfloat16)


def product_kernel(k_local, right_ref, left_ref, out_ref, left_high, left_low, right_high, right_low):
    @pl.when(pl.program_id(0) == 0)
    def _():
        high, low = split(left_ref[...])
        left_high[...] = high
        left_low[...] = low

    rows = right_ref.reshape(right_ref.shape[0] * right_ref.shape[2], LANES)
    stride = k_local * TILES
    for k in range(k_local):
        for t in range(TILES):
            high, low = split(rows[pl.ds(k * TILES + t, V, stride=stride), :])
            right_high[k * V : (k + 1) * V, t * LANES : (t + 1) * LANES] = high
            right_low[k * V : (k + 1) * V, t * LANES : (t + 1) * LANES] = low
    dot = functools.partial(jnp.dot, preferred_element_type=jnp.float32)
    total = dot(left_high[...], right_high[...])
    total += dot(left_high[...], right_low[...])
    total += dot(left_low[...], right_high[...])
    groups, b_local = out_ref.shape[0], out_ref.shape[1]
    total = total.reshape(b_local, groups, NJ // groups, TILES * LANES)
    for group in range(groups):
        out_ref[group] = total[:, group]


def product(right, left, k_local, b_local, groups):
    shards, chunks, rows, _ = right.shape
    width = TILES * LANES
    return pl.pallas_call(
        functools.partial(product_kernel, k_local),
        grid=(chunks,),
        in_specs=[
            pl.BlockSpec((shards, 1, rows, LANES), lambda n: (0, n, 0, 0)),
            pl.BlockSpec(left.shape, lambda n: (0, 0), pipeline_mode=pl.Buffered(1)),
        ],
        out_specs=pl.BlockSpec((groups, b_local, NJ // groups, width), lambda n: (0, 0, 0, n)),
        out_shape=jax.ShapeDtypeStruct((groups, b_local, NJ // groups, chunks * width), jnp.float32),
        scratch_shapes=[
            pltpu.VMEM(left.shape, jnp.bfloat16),
            pltpu.VMEM(left.shape, jnp.bfloat16),
            pltpu.VMEM((left.shape[1], width), jnp.bfloat16),
            pltpu.VMEM((left.shape[1], width), jnp.bfloat16),
        ],
        compiler_params=pltpu.CompilerParams(vmem_limit_bytes=56 * 1024 * 1024),
    )(right, left)


def per_device(amplitudes, integral, residual_in):
    groups = lax.axis_size("row")
    shards = lax.axis_size("col")
    k_local = O // groups
    b_local = integral.shape[0] // NJ
    c_local = amplitudes.shape[0]
    chunks = NI * V // (TILES * LANES)
    rows = c_local * k_local * TILES
    own = amplitudes.reshape(c_local * k_local, chunks, TILES * LANES).transpose(1, 0, 2)
    piece = lax.all_gather(own.reshape(chunks * rows, LANES), "col", axis=0, tiled=True)
    term = product(piece.reshape(shards, chunks, rows, LANES), integral, k_local, b_local, groups)
    block = lax.psum_scatter(term, "row", scatter_dimension=0, tiled=True)
    block = block.reshape(b_local, NJ // groups, NI, V).transpose(0, 2, 1, 3)
    return residual_in + block.reshape(residual_in.shape)


def solution(mesh):
    return jax.shard_map(
        per_device,
        mesh=mesh,
        in_specs=(P("col", "row"), P("col", "row"), P("col", "row")),
        out_specs=P("col", "row"),
        check_vma=False,
    )
```

time: 390 us -> 222 us (0.57)
  local copies, waits for them, and re-layouts: 94.6 us -> 3.92 us
  matrix products: 59.4 us -> 0 us
  waiting for transfers between devices: 219 us -> 178 us
  Pallas kernels: 0 us -> 25.6 us
    dot_general x3 -> x0, local copies, waits for them, and re-layouts: 65.7 us -> none  [per_device(): lax.dot_general(coupling, right, (((1, 2), (1, 0)), ((), ())), precision=...]
    dot_general x1 -> x0, matrix products: 59.4 us -> none  [per_device(): lax.dot_general(coupling, right, (((1, 2), (1, 0)), ((), ())), precision=...]
    all_gather x1, waiting for transfers between devices: 181 us -> 141 us  [per_device(): lax.all_gather(own.reshape(chunks * rows, LANES), 'col', axis=0, tiled=True)]
    pallas_call x0 -> x1, Pallas kernels: none -> 25.6 us  [product(): pl.pallas_call(functools.partial(product_kernel, k_local), grid=(chunks,)...]
    reshape x2 -> x4, local copies, waits for them, and re-layouts: 28.9 us -> 3.72 us  [the longest x1 1.41 us: per_device(): amplitudes.reshape(c_local * k_local, chunks, TILES * LANES)]
  transfers between devices with their start and end apart: 2 -> 2, of which waited for: 2 -> 2; matrix products, arithmetic and copies ran while one was open for 3% -> 0% of each run, Pallas kernels for 0% -> 0%
where the time goes in v1:
time: 222 us
  waiting for transfers between devices  178 us (80%)
  Pallas kernels  25.6 us (12%)
  between operations  13.4 us (6%)
  local copies, waits for them, and re-layouts  3.92 us (2%)
    all_gather x1, waiting for transfers between devices, per_device(): lax.all_gather(own.reshape(chunks * rows, LANES), 'col', axis=0, tiled=True)  141 us
    reduce_scatter x1, waiting for transfers between devices, per_device(): block = lax.psum_scatter(term, 'row', scatter_dimension=0, tiled=True)  37.1 us
    pallas_call x1, Pallas kernels, product(): pl.pallas_call(functools.partial(product_kernel, k_local), grid=(chunks,)...  25.6 us
  transfers between devices with their start and end apart: 2, of which 2 were waited for; matrix products, arithmetic and copies ran while one was open for 0% of the time, Pallas kernels for 0%

profile of v1, /device:TPU:2, one launch (start us, length us, event | category | flops | bytes accessed | tf_op | source)
XLA Modules:
  0.0 221.8 jit_solution(7504119436703645717)
XLA Ops:
  6.5 0.0 all-gather.2.cloned.1.call-start
  6.5 1.4 reshape.15
  7.9 0.2 copy.7
  8.1 0.8 reshape.16
  9.0 0.0 all-gather.2.cloned.1.call-update
  9.0 0.0 reduce-scatter.2.cloned.1.call-start
  9.0 140.9 %all-gather.2.cloned.1.call-done = f32[32000,128]{1,0:T(8,128)} async-done(((f32[1000,128]{1,0:T(8,128)}), f32[32000,128]{1,0:T(8,128)}) %all-gather.2.cloned.1.call-update) | async-done | bytes 16384016 | tf_op jit(solution)/shard_map/all_gather | solution.py:78
  150.0 0.0 copy-start
  150.0 25.6 %shard_map.37 = f32[8,10,8,1280]{3,2,1,0:T(8,128)} custom-call(f32[32,5,200,128]{3,2,1,0:T(8,128)} %bitcast.7, f32[640,3200]{1,0:T(8,128)} %left_ref.1), custom_call_target="tpu_custom_call" | custom-call | tf_op jit(solution)/shard_map/pallas_call | solution.py:50
  175.6 0.0 reduce-scatter.2.cloned.1.call-update
  175.6 37.1 %reduce-scatter.2.cloned.1.call-done = f32[1,10,8,1280]{3,2,1,0:T(8,128)} async-done(((f32[8,10,8,1280]{3,2,1,0:T(8,128)}), f32[1,10,8,1280]{3,2,1,0:T(8,128)}) %reduce-scatter.2.cloned.1.call-update) | async-done | bytes 409616 | tf_op jit(solution)/shard_map/reduce_scatter | solution.py:80
  212.7 1.3 reshape.18
  214.0 0.1 reshape.19
  214.2 0.0 copy-done
  214.2 0.8 add.5
  (1 shorter events, 0.0 us)
Async XLA Ops:
  6.5 143.4 %all-gather.2.cloned.1.call-start = ((), (), s32[]{:S(2)}) async-start(), calls=%async_computation.1 | async-start | bytes 16896000 | tf_op jit(solution)/shard_map/all_gather | solution.py:78
  9.0 203.7 %reduce-scatter.2.cloned.1.call-start = ((), (), s32[]{:S(2)}) async-start(), calls=%async_computation.2 | async-start | bytes 3686400 | tf_op jit(solution)/shard_map/reduce_scatter | solution.py:80
  150.0 64.2 %copy-start = (f32[40,2560]{1,0:T(8,128)S(1)}, f32[40,2560]{1,0:T(8,128)}, u32[]{:S(2)}) copy-start(f32[40,2560]{1,0:T(8,128)} %param.5) | copy-start | bytes 1228804
Sparse Core Ops, SparseCore 0:
  10.0 139.9 all-gather.1
  175.7 36.9 reduce-scatter.1

commit v2 on v0

v2 whole, which is shorter than its diff:
```python
import functools

import jax
import jax.numpy as jnp
from jax import lax
from jax.experimental import pallas as pl
from jax.experimental.pallas import tpu as pltpu
from jax.sharding import PartitionSpec as P

O = 80
V = 320
NI = 4
NJ = 64
LANES = 128
X, Y, Z, CORES = 4, 4, 8, 2
PLAN = (2, 2, 2, 2, 2)

ARRANGE = 160
BLOCK = 320
LIMIT1, LIMIT2 = 56, 32

dot = functools.partial(jnp.dot, preferred_element_type=jnp.float32)


def split(x):
    high = x.astype(jnp.bfloat16)
    return high, (x - high.astype(jnp.float32)).astype(jnp.bfloat16)


def mate(place, core):
    return (place + 1 - 2 * ((place + core) % 2)) % 4


def links(target):
    pairs = []
    for y in range(Y):
        for core in range(CORES):
            for z in range(Z):
                for x in range(X):
                    to_x, to_y, to_z, to_core = target(x, y, z, core)
                    here = ((y * CORES + core) * Z + z) * X + x
                    there = ((to_y * CORES + to_core) * Z + to_z % Z) * X + to_x
                    pairs.append((here, there))
    return pairs


def send(value, target):
    return lax.ppermute(value, ("row", "col"), links(target))


def to_x_mate(x, y, z, c):
    return mate(x, c), y, z, c


def to_x_mate_crossed(x, y, z, c):
    return mate(x, c), y, z, 1 - c


def to_x_other(x, y, z, c):
    return mate(x, 1 - c), y, z, c


def to_y_mate(x, y, z, c):
    return x, mate(y, c), z, c


def to_y_other(x, y, z, c):
    return x, mate(y, 1 - c), z, c


def to_core(x, y, z, c):
    return x, y, z, 1 - c


def up(x, y, z, c):
    return x, y, z + 1, c


def down(x, y, z, c):
    return x, y, z - 1, c


def after(value, *others):
    return lax.optimization_barrier((value, *others))[0]


def turn(k_local, source_ref, left_ref):
    wanted = source_ref.shape[1]
    order = lax.broadcasted_iota(jnp.int32, (V, wanted), 0) == source_ref[...]
    rows = left_ref.shape[0]
    parts = [part[:, k * V : (k + 1) * V] for part in split(left_ref[...]) for k in range(k_local)]
    turned = dot(jnp.concatenate(parts, axis=0), order.astype(jnp.float32).astype(jnp.bfloat16))
    turned = [turned[n * rows : (n + 1) * rows] for n in range(2 * k_local)]
    return turned[:k_local], turned[k_local:]


def keep_kernel(k_local, source_ref, left_ref, high_ref, low_ref):
    high, low = turn(k_local, source_ref, left_ref)
    high_ref[...] = jnp.concatenate(high, axis=1).astype(jnp.bfloat16)
    low_ref[...] = jnp.concatenate(low, axis=1).astype(jnp.bfloat16)


def away_kernel(k_local, source_ref, left_ref, send_ref):
    rows = left_ref.shape[0]
    high, low = turn(k_local, source_ref, left_ref)
    away = jnp.concatenate([a + b for a, b in zip(high, low)], axis=1)
    full = away.shape[1] // LANES
    for t in range(full):
        send_ref[t * rows : (t + 1) * rows, :] = away[:, t * LANES : (t + 1) * LANES]
    rest = away[:, full * LANES :]
    send_ref[full * rows :, :] = jnp.concatenate([rest[: rows // 2], rest[rows // 2 :]], axis=1)


def arrange(kernel, left, source, k_local, blocks, dtype):
    rows, depth = left.shape
    block = ARRANGE
    return pl.pallas_call(
        functools.partial(kernel, k_local),
        grid=(rows // block,),
        in_specs=[pl.BlockSpec(source.shape, lambda m: (0, 0)), pl.BlockSpec((block, depth), lambda m: (m, 0))],
        out_specs=[pl.BlockSpec(shape, lambda m: (m, 0)) for shape in blocks],
        out_shape=[jax.ShapeDtypeStruct((shape[0] * (rows // block), shape[1]), dtype) for shape in blocks],
        compiler_params=pltpu.CompilerParams(vmem_limit_bytes=LIMIT1 * 1024 * 1024),
        cost_estimate=pl.CostEstimate(flops=rows * depth * V * 2, bytes_accessed=rows * depth * 6, transcendentals=0),
    )(source, left)


def product_kernel(k_local, tiles, ringed, place_ref, *refs):
    *pieces, high_ref, low_ref, got_ref, keep_ref, send_ref, right_high, right_low, total_ref = refs
    shared = Z * O // 8
    size = O // 8 * k_local * tiles

    @pl.when(pl.program_id(0) == 0)
    def _():
        if ringed:
            own, other = pieces
            own, other = own.reshape(Z * size, LANES), other
            starts = ((own, 0, size), (other, 0, size))
        else:
            (rows_ref,) = pieces
            starts = ((rows_ref, 0, 2 * size), (rows_ref, size, 2 * size))
        for k in range(k_local):
            for t in range(tiles):
                for half, (ref, start, step) in enumerate(starts):
                    first = start + k * tiles + t
                    if step == size:
                        block = ref[pl.ds(first, shared, stride=k_local * tiles), :]
                    else:
                        block = jnp.concatenate(
                            [ref[pl.ds(first + z * step, O // 8, stride=k_local * tiles), :] for z in range(Z)]
                        )
                    high, low = split(block)
                    at = (2 * k + half) * shared
                    right_high[at : at + shared, t * LANES : (t + 1) * LANES] = high
                    right_low[at : at + shared, t * LANES : (t + 1) * LANES] = low

    rows, depth = high_ref.shape
    full = depth // LANES
    got = []
    for at in range(0, rows * depth // LANES, ARRANGE * depth // LANES):
        blocks = [got_ref[at + t * ARRANGE : at + (t + 1) * ARRANGE, :] for t in range(full)]
        rest = got_ref[at + full * ARRANGE : at + ARRANGE * depth // LANES, :]
        blocks.append(jnp.concatenate([rest[:, : LANES // 2], rest[:, LANES // 2 :]], axis=0))
        got.append(jnp.concatenate(blocks, axis=1))
    got_high, got_low = split(jnp.concatenate(got, axis=0))
    for at, (high, low) in enumerate(((high_ref[...], low_ref[...]), (got_high, got_low))):
        total_ref[...] = dot(high, right_high[...]) + dot(high, right_low[...]) + dot(low, right_high[...])
        for b in range(rows // NJ):
            for out, slots in ((keep_ref, (0, 1)), (send_ref, (2, 3))):
                for slot, which in enumerate(slots):
                    for part in range(CORES):
                        start = pl.multiple_of(b * NJ + place_ref[which * CORES + part] * 8, 8)
                        out[slot, at, b, part * 8 : (part + 1) * 8, :] = total_ref[pl.ds(start, 8), :]


def product(pieces, at, high, low, got, place, k_local, tiles):
    rows, depth = high.shape
    width = tiles * LANES
    block = BLOCK
    b_local = rows // NJ
    ringed = len(pieces) == 2
    left = pl.BlockSpec((block, depth), lambda m, s: (m, 0))
    specs = [pl.BlockSpec(piece.shape, lambda m, s: (0, 0)) for piece in pieces]
    if ringed:
        specs[0] = pl.BlockSpec((Z, 1) + pieces[0].shape[2:], lambda m, s: (0, at, 0, 0))
    away = pl.BlockSpec((block * depth // LANES, LANES), lambda m, s: (m, 0))
    out = pl.BlockSpec((2, 2, block // NJ, 16, width), lambda m, s: (0, 0, m, 0, 0))
    shape = jax.ShapeDtypeStruct((2, 2, b_local, 16, width), jnp.float32)
    return pl.pallas_call(
        functools.partial(product_kernel, k_local, tiles, ringed),
        grid_spec=pltpu.PrefetchScalarGridSpec(
            num_scalar_prefetch=1,
            grid=(rows // block,),
            in_specs=specs + [left, left, away],
            out_specs=[out, out],
            scratch_shapes=[
                pltpu.VMEM((depth, width), jnp.bfloat16),
                pltpu.VMEM((depth, width), jnp.bfloat16),
                pltpu.VMEM((block, width), jnp.float32),
            ],
        ),
        out_shape=[shape, shape],
        compiler_params=pltpu.CompilerParams(vmem_limit_bytes=LIMIT2 * 1024 * 1024),
        cost_estimate=pl.CostEstimate(
            flops=rows * depth * width * 12, bytes_accessed=rows * depth * 12 + rows * width * 16, transcendentals=0
        ),
    )(place, *pieces, high, low, got)


def per_device(amplitudes, integral, residual_in):
    row, col = lax.axis_index("row"), lax.axis_index("col")
    y, core, z, x = row // CORES, row % CORES, col // X, col % X
    k_local = O // lax.axis_size("row")
    c_local = amplitudes.shape[0]
    b_local = integral.shape[0] // NJ

    x_mate, x_other = mate(x, core), mate(x, 1 - core)
    xs = jnp.stack([x, x_other, x_mate, mate(x_mate, 1 - core)])
    zs = jnp.arange(Z)
    source = (zs[None, :, None] * X + xs[:, None, None]) * c_local + jnp.arange(c_local)[None, None, :]
    source = source.reshape(1, V).astype(jnp.int32)
    y_mate, y_other = mate(y, core), mate(y, 1 - core)
    ys = jnp.stack([y, y_other, y_mate, mate(y_mate, 1 - core)])
    place = (ys[:, None] * CORES + jnp.stack([core, 1 - core])[None, :]).reshape(8)
    place = jnp.concatenate([place, z[None]]).astype(jnp.int32)

    blocks, at = [], 0
    for tiles in PLAN:
        part = amplitudes.reshape(c_local * k_local, NI * V)[:, at * LANES : (at + tiles) * LANES]
        blocks.append(part.reshape(c_local * k_local * tiles, LANES))
        at += tiles
    lead, rest = blocks[0], blocks[1:]
    groups = [[q * X + r for q in range(Z)] for r in range(X)]
    gather = functools.partial(lax.all_gather, axis_name="col", axis=0, tiled=True, axis_index_groups=groups)
    gathered = gather(jnp.concatenate(rest)).reshape(Z, -1, LANES)
    pair = jnp.concatenate([lead, send(lead, to_x_other)])
    paired = gather(pair)
    half = V // 2
    packed = (ARRANGE * k_local * half // LANES, LANES)
    (away,) = arrange(away_kernel, integral, source[:, half:], k_local, [packed], jnp.float32)
    got = send(away, to_x_mate)
    natural = (ARRANGE, k_local * half)
    high, low = arrange(keep_kernel, integral, after(source[:, :half], away, pair), k_local, [natural] * 2, jnp.bfloat16)
    gathered = after(gathered, high)
    pieces, at = [], 0
    for block in rest:
        own = gathered[:, at : at + block.shape[0]]
        at += block.shape[0]
        pieces.append([own[:, None], send(own.reshape(-1, LANES), to_x_other)])
    pieces.append([paired])
    plan = PLAN[1:] + PLAN[:1]

    count = len(plan)
    keeps, gives, firsts, seconds = [], [], [], []
    for n in range(count + 2):
        if n < count:
            if n >= 2:
                place = after(place, firsts[n - 2])
            if n >= 3:
                place = after(place, seconds[n - 3])
            keep, give = product(pieces[n], 0, high, low, got, place, k_local, plan[n])
            place = after(place, keep)
            keeps.append(keep)
            gives.append(send(give, to_y_mate))
        if 0 <= n - 1 < count:
            mine = after(keeps[n - 1], keeps[n]) if n < count else keeps[n - 1]
            firsts.append(mine + gives[n - 1])
        if 0 <= n - 2 < count:
            mine = after(firsts[n - 2], keeps[n]) if n < count else firsts[n - 2]
            seconds.append(mine[0] + send(firsts[n - 2][1], to_y_other))
    results = []
    for group in (seconds[:3], seconds[3:]):
        second = jnp.concatenate(group, axis=-1)
        own, mates = second[0], second[1]
        total = own[:, :8] + send(own[:, 8:], to_core)
        total += send(mates[:, :8], to_x_mate)
        total += send(mates[:, 8:], to_x_mate_crossed)
        results.append(total)
    block = jnp.concatenate(results, axis=-1)
    first = PLAN[0] * LANES
    block = jnp.concatenate([block[..., -first:], block[..., :-first]], axis=-1)
    block = block.reshape(b_local, 8, NI, V).transpose(0, 2, 1, 3)
    return residual_in + block.reshape(residual_in.shape)


def solution(mesh):
    return jax.shard_map(
        per_device,
        mesh=mesh,
        in_specs=(P("col", "row"), P("col", "row"), P("col", "row")),
        out_specs=P("col", "row"),
        check_vma=False,
    )
```

time: 390 us -> 178 us (0.46)
  waiting for transfers between devices: 219 us -> 65.8 us
  local copies, waits for them, and re-layouts: 94.6 us -> 14.7 us
  matrix products: 59.4 us -> 0 us
  Pallas kernels: 0 us -> 49.6 us
  starting transfers between devices: 0.04 us -> 25.6 us
    all_gather x1 -> x2, waiting for transfers between devices: 181 us -> 24.2 us  [the longest x1 24.2 us: per_device(): gathered = gather(jnp.concatenate(rest)).reshape(Z, -1, LANES)]
    dot_general x3 -> x0, local copies, waits for them, and re-layouts: 65.7 us -> none  [per_device(): lax.dot_general(coupling, right, (((1, 2), (1, 0)), ((), ())), precision=...]
    dot_general x1 -> x0, matrix products: 59.4 us -> none  [per_device(): lax.dot_general(coupling, right, (((1, 2), (1, 0)), ((), ())), precision=...]
    pallas_call x0 -> x7, Pallas kernels: none -> 49.6 us  [the longest x5 33.5 us: product(): pl.pallas_call(functools.partial(product_kernel, k_local, tiles, ringed),...]
    ppermute x0 -> x22, waiting for transfers between devices: none -> 41.6 us  [send(): return lax.ppermute(value, ('row', 'col'), links(target))]
    reduce_scatter x1 -> x0, waiting for transfers between devices: 37.1 us -> none  [per_device(): cycle_block = lax.psum_scatter(term, 'row', scatter_dimension=1, tiled=True)]
    reshape x2 -> x8, local copies, waits for them, and re-layouts: 28.9 us -> 1.8 us  [the longest x1 1.27 us: per_device(): amplitudes.reshape(c_local * k_local, NI * V)]
    ppermute x0 -> x22, starting transfers between devices: none -> 25.6 us  [send(): return lax.ppermute(value, ('row', 'col'), links(target))]
  transfers between devices with their start and end apart: 2 -> 24, of which waited for: 2 -> 11; matrix products, arithmetic and copies ran while one was open for 3% -> 5% of each run, Pallas kernels for 0% -> 28%
where the time goes in v2:
time: 178 us; the launch traced here: 175 us
  waiting for transfers between devices  65.8 us (37%)
  Pallas kernels  49.6 us (28%)
  starting transfers between devices  25.6 us (14%)
  local copies, waits for them, and re-layouts  14.7 us (8%)
  between operations  13.9 us (8%)
  other arithmetic  5.23 us (3%)
    ppermute x22, waiting for transfers between devices, send(): return lax.ppermute(value, ('row', 'col'), links(target))  41.6 us
    pallas_call x5, Pallas kernels, product(): pl.pallas_call(functools.partial(product_kernel, k_local, tiles, ringed),...  33.5 us
    ppermute x22, starting transfers between devices, send(): return lax.ppermute(value, ('row', 'col'), links(target))  25.6 us
    all_gather x1, waiting for transfers between devices, per_device(): gathered = gather(jnp.concatenate(rest)).reshape(Z, -1, LANES)  24.2 us
    pallas_call x2, Pallas kernels, arrange(): pl.pallas_call(functools.partial(kernel, k_local), grid=(rows // block,),...  16.1 us
    unnamed x19, local copies, waits for them, and re-layouts  7.92 us
    slice x1, local copies, waits for them, and re-layouts, per_device(): own = gathered[:, at:at + block.shape[0]]  3.76 us
  transfers between devices with their start and end apart: 24, of which 11 were waited for; matrix products, arithmetic and copies ran while one was open for 5% of the time, Pallas kernels for 28%

profile of v2, /device:TPU:2, one launch (start us, length us, event | category | flops | bytes accessed | tf_op | source)
XLA Modules:
  0.0 174.7 jit_solution(3175255563724124946)
XLA Ops:
  6.5 1.3 reshape.145
  7.9 0.8 pad_maximum_fusion.2
  8.9 0.1 pad_add_fusion.2
  9.1 0.1 add.220
  9.3 0.6 fusion.14
  9.9 8.2 %shard_map.37 = f32[8000,128]{1,0:T(8,128)} custom-call(s32[1,160]{1,0:T(1,128)} %get-tuple-element.86.source_ref, f32[640,3200]{1,0:T(8,128)} %left_ref.3), custom_call_target="tpu_custom_call" | custom-call | flops 1310720000 | bytes 12288000 | tf_op jit(solution)/shard_map/pallas_call | solution.py:117
  18.1 2.3 %collective-permute-start.2 = (f32[8000,128]{1,0:T(8,128)}, f32[8000,128]{1,0:T(8,128)}, u32[]{:S(2)}, u32[]{:S(2)}) collective-permute-start(f32[8000,128]{1,0:T(8,128)} %shard_map.37), channel_id=1, source_target_pairs={{0,1},{1,0},{2,3},{3,2},{4,5},{5,4},{6,7},{7,6},{8,9},{9,8},{10,11... | collective-permute-start | bytes 12288008 | tf_op jit(solution)/shard_map/ppermute | solution.py:48
  20.4 0.5 collective-permute-start
  20.9 5.4 %collective-permute-done = f32[200,128]{1,0:T(8,128)S(1)} collective-permute-done((f32[200,128]{1,0:T(8,128)S(1)}, f32[200,128]{1,0:T(8,128)S(1)}, u32[]{:S(2)}, u32[]{:S(2)}) %collective-permute-start) | collective-permute-done | bytes 102432 | tf_op jit(solution)/shard_map/ppermute | solution.py:48
  26.4 7.8 %shard_map.38 = (bf16[640,1600]{1,0:T(8,128)(2,1)}, bf16[640,1600]{1,0:T(8,128)(2,1)}) custom-call(s32[1,160]{1,0:T(1,128)} %get-tuple-element.35.source_ref, f32[640,3200]{1,0:T(8,128)} %left_ref.3), custom_call_target="tpu_custom_call" | custom-call | flops 1310720000 | bytes 12288000 | tf_op jit(solution)/shard_map/pallas_call | solution.py:117
  34.2 24.2 %all-gather.3.cloned.1.call-done = f32[6400,128]{1,0:T(8,128)} async-done(((f32[800,128]{1,0:T(8,128)}), f32[6400,128]{1,0:T(8,128)}) %all-gather.3.cloned.1.call-update) | async-done | bytes 3276816 | tf_op jit(solution)/shard_map/all_gather | solution.py:235
  58.3 3.8 %fusion.10 = (f32[8,200,128]{2,1,0:T(8,128)}, f32[8,1,200,128]{3,2,1,0:T(8,128)S(1)}, f32[8,1,200,128]{3,2,1,0:T(8,128)S(1)}, f32[8,1,200,128]{3,2,1,0:T(8,128)S...) fusion(f32[8,800,128]{2,1,0:T(8,128)} %bitcast.65), kind=kLoop, calls=%fused_computation.44 | loop fusion | bytes 9830400 | tf_op jit(solution)/shard_map/slice | solution.py:247
  62.1 1.5 collective-permute-start.1
  63.6 0.1 add_multiply_fusion.1
  63.7 0.6 collective-permute-start.3
  64.4 0.1 add.201
  64.5 0.1 pad_add_fusion.1.place_ref
  64.6 5.0 %collective-permute-done.2.refs_4_.refs_3_ = f32[8000,128]{1,0:T(8,128)} collective-permute-done((f32[8000,128]{1,0:T(8,128)}, f32[8000,128]{1,0:T(8,128)}, u32[]{:S(2)}, u32[]{:S(2)}) %collective-permute-start.2) | collective-permute-done | bytes 4096032 | tf_op jit(solution)/shard_map/ppermute | solution.py:48
  69.6 5.2 %collective-permute-done.1.refs_1_ = f32[1600,128]{1,0:T(8,128)} collective-permute-done((f32[1600,128]{1,0:T(8,128)}, f32[1600,128]{1,0:T(8,128)}, u32[]{:S(2)}, u32[]{:S(2)}) %collective-permute-start.1) | collective-permute-done | bytes 819232 | tf_op jit(solution)/shard_map/ppermute | solution.py:48
  74.8 1.7 copy-done
  76.4 1.6 copy-done.2
  78.0 6.8 %shard_map.39 = (f32[2,2,10,16,256]{4,3,2,1,0:T(8,128)S(1)}, f32[2,2,10,16,256]{4,3,2,1,0:T(8,128)S(1)}) custom-call(s32[9]{0:T(128)S(1)} %pad_add_fusion.1.place_ref, f32[8,1,200,128]{3,2,1,0:T(8,128)S(1)} %get-tuple-element.66.refs_0_, f32[1600,128]{1,0:T(8,128)} %collective-permute-done.1.refs_1_, bf16[640,1600]{1,0:T(8,128)(2,1)S(1)} %copy-done, ...), custom_call_target="tpu_custom_call" | custom-call | flops 3145728000 | bytes 14909440 | tf_op jit(solution)/shard_map/pallas_call | solution.py:189
  84.8 1.6 collective-permute-start.4
  86.4 1.5 collective-permute-start.5
  87.9 6.8 %shard_map.40 = (f32[2,2,10,16,256]{4,3,2,1,0:T(8,128)S(1)}, f32[2,2,10,16,256]{4,3,2,1,0:T(8,128)S(1)}) custom-call(s32[9]{0:T(128)S(1)} %pad_add_fusion.1.place_ref, f32[8,1,200,128]{3,2,1,0:T(8,128)S(1)} %get-tuple-element.67.refs_0_, f32[1600,128]{1,0:T(8,128)} %collective-permute-done.3.refs_1_, bf16[640,1600]{1,0:T(8,128)(2,1)S(1)} %copy-done, ...), custom_call_target="tpu_custom_call" | custom-call | flops 3145728000 | bytes 14909440 | tf_op jit(solution)/shard_map/pallas_call | solution.py:189
  94.7 0.6 collective-permute-start.6
  95.3 0.5 collective-permute-start.8
  95.9 0.1 add.221
  96.0 3.2 %collective-permute-start.7 = (f32[2,10,16,256]{3,2,1,0:T(8,128)S(1)}, f32[2,10,16,256]{3,2,1,0:T(8,128)S(1)}, u32[]{:S(2)}, u32[]{:S(2)}) collective-permute-start(f32[2,10,16,256]{3,2,1,0:T(8,128)S(1)} %slice_bitcast_fusion.8), channel_id=1, source_target_pairs={{0,192},{1,193},{2,194},{3,195},{4,196},{5,197},{6,198},{7,199},{8... | collective-permute-start | bytes 983048 | tf_op jit(solution)/shard_map/ppermute | solution.py:48
  99.2 6.6 %shard_map.41 = (f32[2,2,10,16,256]{4,3,2,1,0:T(8,128)S(1)}, f32[2,2,10,16,256]{4,3,2,1,0:T(8,128)S(1)}) custom-call(s32[9]{0:T(128)S(1)} %pad_add_fusion.1.place_ref, f32[8,1,200,128]{3,2,1,0:T(8,128)S(1)} %get-tuple-element.68.refs_0_, f32[1600,128]{1,0:T(8,128)S(1)} %collective-permute-done.5.refs_1_, bf16[640,1600]{1,0:T(8,128)(2,1)S(1)} %copy-done, ...), custom_call_target="tpu_custom_call" | custom-call | flops 3145728000 | bytes 14909440 | tf_op jit(solution)/shard_map/pallas_call | solution.py:189
  105.8 3.1 %collective-permute-done.6 = f32[2,2,10,16,256]{4,3,2,1,0:T(8,128)S(1)} collective-permute-done((f32[2,2,10,16,256]{4,3,2,1,0:T(8,128)S(1)}, f32[2,2,10,16,256]{4,3,2,1,0:T(8,128)S(1)}, u32[]{:S(2)}, u32[]{:S(2)}) %collective-permute-start.6) | collective-permute-done | bytes 655392 | tf_op jit(solution)/shard_map/ppermute | solution.py:48
  108.9 0.1 add.222
  109.0 0.6 collective-permute-start.9
  109.6 3.0 %collective-permute-start.10 = (f32[2,10,16,256]{3,2,1,0:T(8,128)S(1)}, f32[2,10,16,256]{3,2,1,0:T(8,128)S(1)}, u32[]{:S(2)}, u32[]{:S(2)}) collective-permute-start(f32[2,10,16,256]{3,2,1,0:T(8,128)S(1)} %slice_bitcast_fusion.7), channel_id=1, source_target_pairs={{0,192},{1,193},{2,194},{3,195},{4,196},{5,197},{6,198},{7,199},{8... | collective-permute-start | bytes 983048 | tf_op jit(solution)/shard_map/ppermute | solution.py:48
  112.7 6.6 %shard_map.42 = (f32[2,2,10,16,256]{4,3,2,1,0:T(8,128)S(1)}, f32[2,2,10,16,256]{4,3,2,1,0:T(8,128)S(1)}) custom-call(s32[9]{0:T(128)S(1)} %pad_add_fusion.1.place_ref, f32[8,1,200,128]{3,2,1,0:T(8,128)S(1)} %get-tuple-element.69.refs_0_, f32[1600,128]{1,0:T(8,128)S(1)} %collective-permute-done.8.refs_1_, bf16[640,1600]{1,0:T(8,128)(2,1)S(1)} %copy-done, ...), custom_call_target="tpu_custom_call" | custom-call | flops 3145728000 | bytes 14909440 | tf_op jit(solution)/shard_map/pallas_call | solution.py:189
  119.3 0.3 collective-permute-start.11
  119.5 1.9 %collective-permute-done.10 = f32[2,10,16,256]{3,2,1,0:T(8,128)S(1)} collective-permute-done((f32[2,10,16,256]{3,2,1,0:T(8,128)S(1)}, f32[2,10,16,256]{3,2,1,0:T(8,128)S(1)}, u32[]{:S(2)}, u32[]{:S(2)}) %collective-permute-start.10) | collective-permute-done | bytes 327712 | tf_op jit(solution)/shard_map/ppermute | solution.py:48
  121.5 1.7 collective-permute-done.9
  123.2 0.1 add.224
  123.3 2.3 %collective-permute-start.18 = (f32[2,10,16,256]{3,2,1,0:T(8,128)S(1)}, f32[2,10,16,256]{3,2,1,0:T(8,128)}, u32[]{:S(2)}, u32[]{:S(2)}) collective-permute-start(f32[2,10,16,256]{3,2,1,0:T(8,128)S(1)} %slice_bitcast_fusion.2), channel_id=1, source_target_pairs={{0,192},{1,193},{2,194},{3,195},{4,196},{5,197},{6,198},{7,199},{8... | collective-permute-start | bytes 983048 | tf_op jit(solution)/shard_map/ppermute | solution.py:48
  125.6 1.6 copy-done.1
  127.2 1.6 copy-done.3
  128.8 1.4 copy-done.4
  130.2 6.7 %shard_map.43 = (f32[2,2,10,16,256]{4,3,2,1,0:T(8,128)S(1)}, f32[2,2,10,16,256]{4,3,2,1,0:T(8,128)S(1)}) custom-call(s32[9]{0:T(128)S(1)} %pad_add_fusion.1.place_ref, f32[3200,128]{1,0:T(8,128)S(1)} %copy-done.4, bf16[640,1600]{1,0:T(8,128)(2,1)S(1)} %copy-done.1, bf16[640,1600]{1,0:T(8,128)(2,1)S(1)} %copy-done.3, ...), custom_call_target="tpu_custom_call" | custom-call | flops 3145728000 | bytes 14909440 | tf_op jit(solution)/shard_map/pallas_call | solution.py:189
  136.9 0.7 collective-permute-start.13
  137.7 1.2 add.226
  138.9 0.7 collective-permute-start.12
  139.6 1.0 bitcast_add_fusion
  140.8 10.3 %collective-permute-done.13 = f32[2,2,10,16,256]{4,3,2,1,0:T(8,128)S(1)} collective-permute-done((f32[2,2,10,16,256]{4,3,2,1,0:T(8,128)S(1)}, f32[2,2,10,16,256]{4,3,2,1,0:T(8,128)S(1)}, u32[]{:S(2)}, u32[]{:S(2)}) %collective-permute-start.13) | collective-permute-done | bytes 655392 | tf_op jit(solution)/shard_map/ppermute | solution.py:48
  151.1 0.1 add.228
  151.2 1.1 collective-permute-start.14
  152.4 0.1 collective-permute-start.21
  152.5 2.2 %collective-permute-start.20 = (f32[10,8,768]{2,1,0:T(8,128)S(1)}, f32[10,8,768]{2,1,0:T(8,128)S(1)}, u32[]{:S(2)}, u32[]{:S(2)}) collective-permute-start(f32[10,8,768]{2,1,0:T(8,128)S(1)} %get-tuple-element.82), channel_id=1, source_target_pairs={{0,1},{1,0},{2,3},{3,2},{4,5},{5,4},{6,7},{7,6},{8,9},{9,8},{10,11... | collective-permute-start | bytes 737288 | tf_op jit(solution)/shard_map/ppermute | solution.py:48
  154.8 0.3 collective-permute-start.19
  155.2 4.5 %collective-permute-done.14 = f32[2,10,16,256]{3,2,1,0:T(8,128)S(1)} collective-permute-done((f32[2,10,16,256]{3,2,1,0:T(8,128)S(1)}, f32[2,10,16,256]{3,2,1,0:T(8,128)S(1)}, u32[]{:S(2)}, u32[]{:S(2)}) %collective-permute-start.14) | collective-permute-done | bytes 327712 | tf_op jit(solution)/shard_map/ppermute | solution.py:48
  159.7 0.1 fusion.2
  159.8 0.1 collective-permute-start.17
  159.9 1.6 collective-permute-start.16
  161.5 0.3 collective-permute-start.15
  161.9 2.7 %collective-permute-done.17 = f32[10,8,512]{2,1,0:T(8,128)S(1)} collective-permute-done((f32[10,8,512]{2,1,0:T(8,128)S(1)}, f32[10,8,512]{2,1,0:T(8,128)S(1)}, u32[]{:S(2)}, u32[]{:S(2)}) %collective-permute-start.17) | collective-permute-done | bytes 163872 | tf_op jit(solution)/shard_map/ppermute | solution.py:48
  164.6 1.8 %collective-permute-done.16 = f32[10,8,512]{2,1,0:T(8,128)S(1)} collective-permute-done((f32[10,8,512]{2,1,0:T(8,128)S(1)}, f32[10,8,512]{2,1,0:T(8,128)S(1)}, u32[]{:S(2)}, u32[]{:S(2)}) %collective-permute-start.16) | collective-permute-done | bytes 163872 | tf_op jit(solution)/shard_map/ppermute | solution.py:48
  166.6 0.4 reshape.156
  166.9 0.1 reshape.157
  167.1 0.8 add.237
  (63 shorter events, 1.2 us)
Async XLA Ops:
  6.5 51.8 %all-gather.3.cloned.1.call-start = ((), (), s32[]{:S(2)}) async-start(), calls=%async_computation | async-start | bytes 3686400 | tf_op jit(solution)/shard_map/all_gather | solution.py:235
  8.7 116.8 %all-gather.5.cloned.1.call-start = ((), (), s32[]{:S(2)}) async-start(), calls=%async_computation.1 | async-start | bytes 1843200 | tf_op jit(solution)/shard_map/all_gather | solution.py:237
  18.1 51.5 %collective-permute-start.2 = (f32[8000,128]{1,0:T(8,128)}, f32[8000,128]{1,0:T(8,128)}, u32[]{:S(2)}, u32[]{:S(2)}) collective-permute-start(f32[8000,128]{1,0:T(8,128)} %shard_map.37), channel_id=1, source_target_pairs={{0,1},{1,0},{2,3},{3,2},{4,5},{5,4},{6,7},{7,6},{8,9},{9,8},{10,11... | collective-permute-start | bytes 12288008 | tf_op jit(solution)/shard_map/ppermute | solution.py:48
  20.4 5.9 %collective-permute-start = (f32[200,128]{1,0:T(8,128)S(1)}, f32[200,128]{1,0:T(8,128)S(1)}, u32[]{:S(2)}, u32[]{:S(2)}) collective-permute-start(f32[200,128]{1,0:T(8,128)S(1)} %reshape.151), channel_id=1, source_target_pairs={{0,3},{1,2},{2,1},{3,0},{4,7},{5,6},{6,5},{7,4},{8,11},{9,10},{10,... | collective-permute-start | bytes 307208 | tf_op jit(solution)/shard_map/ppermute | solution.py:48
  26.3 7.8 %copy-start.7 = (f32[400,128]{1,0:T(8,128)}, f32[400,128]{1,0:T(8,128)S(1)}, u32[]{:S(2)}) copy-start(f32[400,128]{1,0:T(8,128)S(1)} %constant_dynamic-update-slice_fusion) | copy-start | bytes 614404
  62.1 12.7 %collective-permute-start.1 = (f32[1600,128]{1,0:T(8,128)}, f32[1600,128]{1,0:T(8,128)}, u32[]{:S(2)}, u32[]{:S(2)}) collective-permute-start(f32[1600,128]{1,0:T(8,128)} %bitcast.14), channel_id=1, source_target_pairs={{0,3},{1,2},{2,1},{3,0},{4,7},{5,6},{6,5},{7,4},{8,11},{9,10},{10,... | collective-permute-start | bytes 2457608 | tf_op jit(solution)/shard_map/ppermute | solution.py:48
  63.7 24.1 %collective-permute-start.3 = (f32[1600,128]{1,0:T(8,128)}, f32[1600,128]{1,0:T(8,128)}, u32[]{:S(2)}, u32[]{:S(2)}) collective-permute-start(f32[1600,128]{1,0:T(8,128)} %bitcast.69), channel_id=1, source_target_pairs={{0,3},{1,2},{2,1},{3,0},{4,7},{5,6},{6,5},{7,4},{8,11},{9,10},{10,... | collective-permute-start | bytes 2457608 | tf_op jit(solution)/shard_map/ppermute | solution.py:48
  74.8 1.7 copy-start
  76.4 1.6 copy-start.2
  78.0 8.4 %copy-start.6 = (f32[8,200,128]{2,1,0:T(8,128)S(1)}, f32[8,200,128]{2,1,0:T(8,128)}, u32[]{:S(2)}) copy-start(f32[8,200,128]{2,1,0:T(8,128)} %get-tuple-element.70) | copy-start | bytes 2457604
  84.8 11.0 %collective-permute-start.4 = (f32[2,2,10,16,256]{4,3,2,1,0:T(8,128)S(1)}, f32[2,2,10,16,256]{4,3,2,1,0:T(8,128)S(1)}, u32[]{:S(2)}, u32[]{:S(2)}) collective-permute-start(f32[2,2,10,16,256]{4,3,2,1,0:T(8,128)S(1)} %get-tuple-element.44), channel_id=1, source_target_pairs={{0,64},{1,65},{2,66},{3,67},{4,68},{5,69},{6,70},{7,71},{8,72},{9,... | collective-permute-start | bytes 1966088 | tf_op jit(solution)/shard_map/ppermute | solution.py:48
  86.4 12.8 %collective-permute-start.5 = (f32[1600,128]{1,0:T(8,128)S(1)}, f32[1600,128]{1,0:T(8,128)S(1)}, u32[]{:S(2)}, u32[]{:S(2)}) collective-permute-start(f32[1600,128]{1,0:T(8,128)S(1)} %bitcast.68), channel_id=1, source_target_pairs={{0,3},{1,2},{2,1},{3,0},{4,7},{5,6},{6,5},{7,4},{8,11},{9,10},{10,... | collective-permute-start | bytes 2457608 | tf_op jit(solution)/shard_map/ppermute | solution.py:48
  87.9 7.5 %copy-start.5 = (f32[8,200,128]{2,1,0:T(8,128)S(1)}, f32[8,200,128]{2,1,0:T(8,128)}, u32[]{:S(2)}) copy-start(f32[8,200,128]{2,1,0:T(8,128)} %get-tuple-element.65) | copy-start | bytes 2457604
  94.7 14.2 %collective-permute-start.6 = (f32[2,2,10,16,256]{4,3,2,1,0:T(8,128)S(1)}, f32[2,2,10,16,256]{4,3,2,1,0:T(8,128)S(1)}, u32[]{:S(2)}, u32[]{:S(2)}) collective-permute-start(f32[2,2,10,16,256]{4,3,2,1,0:T(8,128)S(1)} %get-tuple-element.49), channel_id=1, source_target_pairs={{0,64},{1,65},{2,66},{3,67},{4,68},{5,69},{6,70},{7,71},{8,72},{9,... | collective-permute-start | bytes 1966088 | tf_op jit(solution)/shard_map/ppermute | solution.py:48
  95.3 17.3 %collective-permute-start.8 = (f32[1600,128]{1,0:T(8,128)S(1)}, f32[1600,128]{1,0:T(8,128)S(1)}, u32[]{:S(2)}, u32[]{:S(2)}) collective-permute-start(f32[1600,128]{1,0:T(8,128)S(1)} %bitcast.67), channel_id=1, source_target_pairs={{0,3},{1,2},{2,1},{3,0},{4,7},{5,6},{6,5},{7,4},{8,11},{9,10},{10,... | collective-permute-start | bytes 2457608 | tf_op jit(solution)/shard_map/ppermute | solution.py:48
  96.0 16.6 %collective-permute-start.7 = (f32[2,10,16,256]{3,2,1,0:T(8,128)S(1)}, f32[2,10,16,256]{3,2,1,0:T(8,128)S(1)}, u32[]{:S(2)}, u32[]{:S(2)}) collective-permute-start(f32[2,10,16,256]{3,2,1,0:T(8,128)S(1)} %slice_bitcast_fusion.8), channel_id=1, source_target_pairs={{0,192},{1,193},{2,194},{3,195},{4,196},{5,197},{6,198},{7,199},{8... | collective-permute-start | bytes 983048 | tf_op jit(solution)/shard_map/ppermute | solution.py:48
  109.0 14.2 %collective-permute-start.9 = (f32[2,2,10,16,256]{4,3,2,1,0:T(8,128)S(1)}, f32[2,2,10,16,256]{4,3,2,1,0:T(8,128)S(1)}, u32[]{:S(2)}, u32[]{:S(2)}) collective-permute-start(f32[2,2,10,16,256]{4,3,2,1,0:T(8,128)S(1)} %get-tuple-element.56), channel_id=1, source_target_pairs={{0,64},{1,65},{2,66},{3,67},{4,68},{5,69},{6,70},{7,71},{8,72},{9,... | collective-permute-start | bytes 1966088 | tf_op jit(solution)/shard_map/ppermute | solution.py:48
  109.6 11.8 %collective-permute-start.10 = (f32[2,10,16,256]{3,2,1,0:T(8,128)S(1)}, f32[2,10,16,256]{3,2,1,0:T(8,128)S(1)}, u32[]{:S(2)}, u32[]{:S(2)}) collective-permute-start(f32[2,10,16,256]{3,2,1,0:T(8,128)S(1)} %slice_bitcast_fusion.7), channel_id=1, source_target_pairs={{0,192},{1,193},{2,194},{3,195},{4,196},{5,197},{6,198},{7,199},{8... | collective-permute-start | bytes 983048 | tf_op jit(solution)/shard_map/ppermute | solution.py:48
  119.3 18.4 %collective-permute-start.11 = (f32[2,2,10,16,256]{4,3,2,1,0:T(8,128)S(1)}, f32[2,2,10,16,256]{4,3,2,1,0:T(8,128)}, u32[]{:S(2)}, u32[]{:S(2)}) collective-permute-start(f32[2,2,10,16,256]{4,3,2,1,0:T(8,128)S(1)} %get-tuple-element.62), channel_id=1, source_target_pairs={{0,64},{1,65},{2,66},{3,67},{4,68},{5,69},{6,70},{7,71},{8,72},{9,... | collective-permute-start | bytes 1966088 | tf_op jit(solution)/shard_map/ppermute | solution.py:48
  123.3 16.3 %collective-permute-start.18 = (f32[2,10,16,256]{3,2,1,0:T(8,128)S(1)}, f32[2,10,16,256]{3,2,1,0:T(8,128)}, u32[]{:S(2)}, u32[]{:S(2)}) collective-permute-start(f32[2,10,16,256]{3,2,1,0:T(8,128)S(1)} %slice_bitcast_fusion.2), channel_id=1, source_target_pairs={{0,192},{1,193},{2,194},{3,195},{4,196},{5,197},{6,198},{7,199},{8... | collective-permute-start | bytes 983048 | tf_op jit(solution)/shard_map/ppermute | solution.py:48
  125.6 1.6 copy-start.1
  127.2 1.6 copy-start.3
  128.8 1.4 copy-start.4
  136.9 14.2 %collective-permute-start.13 = (f32[2,2,10,16,256]{4,3,2,1,0:T(8,128)S(1)}, f32[2,2,10,16,256]{4,3,2,1,0:T(8,128)S(1)}, u32[]{:S(2)}, u32[]{:S(2)}) collective-permute-start(f32[2,2,10,16,256]{4,3,2,1,0:T(8,128)S(1)} %get-tuple-element.63), channel_id=1, source_target_pairs={{0,64},{1,65},{2,66},{3,67},{4,68},{5,69},{6,70},{7,71},{8,72},{9,... | collective-permute-start | bytes 1966088 | tf_op jit(solution)/shard_map/ppermute | solution.py:48
  138.9 16.2 %collective-permute-start.12 = (f32[2,10,16,256]{3,2,1,0:T(8,128)S(1)}, f32[2,10,16,256]{3,2,1,0:T(8,128)S(1)}, u32[]{:S(2)}, u32[]{:S(2)}) collective-permute-start(f32[2,10,16,256]{3,2,1,0:T(8,128)S(1)} %slice_bitcast_fusion.5), channel_id=1, source_target_pairs={{0,192},{1,193},{2,194},{3,195},{4,196},{5,197},{6,198},{7,199},{8... | collective-permute-start | bytes 983048 | tf_op jit(solution)/shard_map/ppermute | solution.py:48
  151.2 8.4 %collective-permute-start.14 = (f32[2,10,16,256]{3,2,1,0:T(8,128)S(1)}, f32[2,10,16,256]{3,2,1,0:T(8,128)S(1)}, u32[]{:S(2)}, u32[]{:S(2)}) collective-permute-start(f32[2,10,16,256]{3,2,1,0:T(8,128)S(1)} %slice_bitcast_fusion.3), channel_id=1, source_target_pairs={{0,192},{1,193},{2,194},{3,195},{4,196},{5,197},{6,198},{7,199},{8... | collective-permute-start | bytes 983048 | tf_op jit(solution)/shard_map/ppermute | solution.py:48
  152.4 9.1 %collective-permute-start.21 = (f32[10,8,768]{2,1,0:T(8,128)S(1)}, f32[10,8,768]{2,1,0:T(8,128)S(1)}, u32[]{:S(2)}, u32[]{:S(2)}) collective-permute-start(f32[10,8,768]{2,1,0:T(8,128)S(1)} %get-tuple-element.83), channel_id=1, source_target_pairs={{0,33},{1,32},{2,35},{3,34},{4,37},{5,36},{6,39},{7,38},{8,41},{9,... | collective-permute-start | bytes 737288 | tf_op jit(solution)/shard_map/ppermute | solution.py:48
  152.5 9.3 %collective-permute-start.20 = (f32[10,8,768]{2,1,0:T(8,128)S(1)}, f32[10,8,768]{2,1,0:T(8,128)S(1)}, u32[]{:S(2)}, u32[]{:S(2)}) collective-permute-start(f32[10,8,768]{2,1,0:T(8,128)S(1)} %get-tuple-element.82), channel_id=1, source_target_pairs={{0,1},{1,0},{2,3},{3,2},{4,5},{5,4},{6,7},{7,6},{8,9},{9,8},{10,11... | collective-permute-start | bytes 737288 | tf_op jit(solution)/shard_map/ppermute | solution.py:48
  154.8 7.1 %collective-permute-start.19 = (f32[10,8,768]{2,1,0:T(8,128)S(1)}, f32[10,8,768]{2,1,0:T(8,128)S(1)}, u32[]{:S(2)}, u32[]{:S(2)}) collective-permute-start(f32[10,8,768]{2,1,0:T(8,128)S(1)} %slice.163), channel_id=1, source_target_pairs={{0,32},{1,33},{2,34},{3,35},{4,36},{5,37},{6,38},{7,39},{8,40},{9,... | collective-permute-start | bytes 737288 | tf_op jit(solution)/shard_map/ppermute | solution.py:48
  159.8 7.3 %copy-start.8 = (f32[40,2560]{1,0:T(8,128)S(1)}, f32[40,2560]{1,0:T(8,128)}, u32[]{:S(2)}) copy-start(f32[40,2560]{1,0:T(8,128)} %param.5) | copy-start | bytes 1228804
  159.8 4.8 %collective-permute-start.17 = (f32[10,8,512]{2,1,0:T(8,128)S(1)}, f32[10,8,512]{2,1,0:T(8,128)S(1)}, u32[]{:S(2)}, u32[]{:S(2)}) collective-permute-start(f32[10,8,512]{2,1,0:T(8,128)S(1)} %get-tuple-element.85), channel_id=1, source_target_pairs={{0,33},{1,32},{2,35},{3,34},{4,37},{5,36},{6,39},{7,38},{8,41},{9,... | collective-permute-start | bytes 491528 | tf_op jit(solution)/shard_map/ppermute | solution.py:48
  159.9 6.6 %collective-permute-start.16 = (f32[10,8,512]{2,1,0:T(8,128)S(1)}, f32[10,8,512]{2,1,0:T(8,128)S(1)}, u32[]{:S(2)}, u32[]{:S(2)}) collective-permute-start(f32[10,8,512]{2,1,0:T(8,128)S(1)} %get-tuple-element.84), channel_id=1, source_target_pairs={{0,1},{1,0},{2,3},{3,2},{4,5},{5,4},{6,7},{7,6},{8,9},{9,8},{10,11... | collective-permute-start | bytes 491528 | tf_op jit(solution)/shard_map/ppermute | solution.py:48
  161.5 4.9 %collective-permute-start.15 = (f32[10,8,512]{2,1,0:T(8,128)S(1)}, f32[10,8,512]{2,1,0:T(8,128)S(1)}, u32[]{:S(2)}, u32[]{:S(2)}) collective-permute-start(f32[10,8,512]{2,1,0:T(8,128)S(1)} %slice.156), channel_id=1, source_target_pairs={{0,32},{1,33},{2,34},{3,35},{4,36},{5,37},{6,38},{7,39},{8,40},{9,... | collective-permute-start | bytes 491528 | tf_op jit(solution)/shard_map/ppermute | solution.py:48
Sparse Core Ops, SparseCore 0:
  9.1 49.1 all-gather.2
  64.6 39.6 all-gather.4

commit v3 on v2

--- a/solution.py
+++ b/solution.py
@@ -15,8 +15,9 @@
 X, Y, Z, CORES = 4, 4, 8, 2
 PLAN = (2, 2, 2, 2, 2)
 
-ARRANGE = 160
+ARRANGE = 320
 BLOCK = 320
+LAST = 2
 LIMIT1, LIMIT2 = 56, 32
 
 dot = functools.partial(jnp.dot, preferred_element_type=jnp.float32)
@@ -66,6 +67,18 @@
 
 def to_y_other(x, y, z, c):
     return x, mate(y, 1 - c), z, c
+
+
+def to_y_other_crossed(x, y, z, c):
+    return x, mate(y, 1 - c), z, 1 - c
+
+
+def to_corner(x, y, z, c):
+    return mate(x, c), mate(y, 1 - c), z, c
+
+
+def to_corner_crossed(x, y, z, c):
+    return mate(x, c), mate(y, 1 - c), z, 1 - c
 
 
 def to_core(x, y, z, c):
@@ -202,7 +215,7 @@
         out_shape=[shape, shape],
         compiler_params=pltpu.CompilerParams(vmem_limit_bytes=LIMIT2 * 1024 * 1024),
         cost_estimate=pl.CostEstimate(
-            flops=rows * depth * width * 12, bytes_accessed=rows * depth * 12 + rows * width * 16, transcendentals=0
+            flops=rows * width, bytes_accessed=rows * width, transcendentals=0
         ),
     )(place, *pieces, high, low, got)
 
@@ -244,20 +257,22 @@
     gathered = after(gathered, high)
     pieces, at = [], 0
     for block in rest:
+        if pieces:
+            gathered = after(gathered, outgoing)
         own = gathered[:, at : at + block.shape[0]]
         at += block.shape[0]
-        pieces.append([own[:, None], send(own.reshape(-1, LANES), to_x_other)])
+        outgoing = own.reshape(-1, LANES)
+        pieces.append([own[:, None], send(outgoing, to_x_other)])
     pieces.append([paired])
+    place = after(place, outgoing)
     plan = PLAN[1:] + PLAN[:1]
 
     count = len(plan)
-    keeps, gives, firsts, seconds = [], [], [], []
-    for n in range(count + 2):
+    keeps, gives, firsts, halves, seconds = [], [], [], [], []
+    for n in range(count + 3):
         if n < count:
             if n >= 2:
                 place = after(place, firsts[n - 2])
-            if n >= 3:
-                place = after(place, seconds[n - 3])
             keep, give = product(pieces[n], 0, high, low, got, place, k_local, plan[n])
             place = after(place, keep)
             keeps.append(keep)
@@ -265,16 +280,32 @@
         if 0 <= n - 1 < count:
             mine = after(keeps[n - 1], keeps[n]) if n < count else keeps[n - 1]
             firsts.append(mine + gives[n - 1])
-        if 0 <= n - 2 < count:
-            mine = after(firsts[n - 2], keeps[n]) if n < count else firsts[n - 2]
-            seconds.append(mine[0] + send(firsts[n - 2][1], to_y_other))
+        if 0 <= n - 2 < count - LAST:
+            halves.append(send(firsts[n - 2][1], to_y_other))
+        if 0 <= n - 3 < count - LAST:
+            mine = after(firsts[n - 3], keeps[n]) if n < count else firsts[n - 3]
+            seconds.append(mine[0] + halves[n - 3])
     results = []
-    for group in (seconds[:3], seconds[3:]):
-        second = jnp.concatenate(group, axis=-1)
+    for group in (seconds,):
+        second = after(jnp.concatenate(group, axis=-1), keeps[-1])
         own, mates = second[0], second[1]
         total = own[:, :8] + send(own[:, 8:], to_core)
         total += send(mates[:, :8], to_x_mate)
         total += send(mates[:, 8:], to_x_mate_crossed)
+        results.append(total)
+    if LAST:
+        (own, mates), (own_far, mates_far) = jnp.concatenate(firsts[-LAST:], axis=-1)
+        total = own[:, :8]
+        for value, target in (
+            (own_far[:, :8], to_y_other),
+            (own_far[:, 8:], to_y_other_crossed),
+            (mates_far[:, :8], to_corner),
+            (mates_far[:, 8:], to_corner_crossed),
+            (mates[:, :8], to_x_mate),
+            (mates[:, 8:], to_x_mate_crossed),
+            (own[:, 8:], to_core),
+        ):
+            total += send(value, target)
         results.append(total)
     block = jnp.concatenate(results, axis=-1)
     first = PLAN[0] * LANES

time: 178 us -> 168 us (0.944)
  waiting for transfers between devices: 65.8 us -> 43 us
  starting transfers between devices: 25.6 us -> 33.7 us
  local copies, waits for them, and re-layouts: 14.7 us -> 17.8 us
    ppermute x22 -> x24, waiting for transfers between devices: 41.6 us -> 18.2 us  [send(): return lax.ppermute(value, ('row', 'col'), links(target))]
    ppermute x22 -> x24, starting transfers between devices: 25.6 us -> 33.7 us  [send(): return lax.ppermute(value, ('row', 'col'), links(target))]
    broadcast_in_dim x0 -> x4, local copies, waits for them, and re-layouts: none -> 7.2 us  [per_device(): pieces.append([own[:, None], send(outgoing, to_x_other)])]
    slice x1 -> x4, local copies, waits for them, and re-layouts: 3.76 us -> 0.09 us  [the longest x1 0.03 us: per_device(): own_far[:, :8]]
    unnamed x19 -> x21, local copies, waits for them, and re-layouts: 7.92 us -> 6.15 us
  transfers between devices with their start and end apart: 24 -> 26, of which waited for: 11 -> 11; matrix products, arithmetic and copies ran while one was open for 5% -> 9% of each run, Pallas kernels for 28% -> 30%
where the time goes in v3:
time: 168 us; the launch traced here: 165 us
  Pallas kernels  49.2 us (29%)
  waiting for transfers between devices  43 us (26%)
  starting transfers between devices  33.7 us (20%)
  local copies, waits for them, and re-layouts  17.8 us (11%)
  between operations  13.9 us (8%)
  other arithmetic  7 us (4%)
    pallas_call x5, Pallas kernels, product(): pl.pallas_call(functools.partial(product_kernel, k_local, tiles, ringed),...  34.4 us
    ppermute x24, starting transfers between devices, send(): return lax.ppermute(value, ('row', 'col'), links(target))  33.7 us
    all_gather x1, waiting for transfers between devices, per_device(): gathered = gather(jnp.concatenate(rest)).reshape(Z, -1, LANES)  24.7 us
    ppermute x24, waiting for transfers between devices, send(): return lax.ppermute(value, ('row', 'col'), links(target))  18.2 us
    pallas_call x2, Pallas kernels, arrange(): pl.pallas_call(functools.partial(kernel, k_local), grid=(rows // block,),...  14.8 us
    broadcast_in_dim x4, local copies, waits for them, and re-layouts, per_device(): pieces.append([own[:, None], send(outgoing, to_x_other)])  7.2 us
    unnamed x21, local copies, waits for them, and re-layouts  6.15 us
  transfers between devices with their start and end apart: 26, of which 11 were waited for; matrix products, arithmetic and copies ran while one was open for 9% of the time, Pallas kernels for 30%

profile of v3, /device:TPU:2, one launch (start us, length us, event | category | flops | bytes accessed | tf_op | source)
XLA Modules:
  0.0 164.7 jit_solution(14651571923225732959)
XLA Ops:
  6.5 1.3 reshape.153
  7.9 0.8 pad_maximum_fusion.2
  9.3 0.7 fusion.22
  9.9 7.6 %shard_map.37 = f32[8000,128]{1,0:T(8,128)} custom-call(s32[1,160]{1,0:T(1,128)} %get-tuple-element.96.source_ref, f32[640,3200]{1,0:T(8,128)} %left_ref.3), custom_call_target="tpu_custom_call" | custom-call | flops 1310720000 | bytes 12288000 | tf_op jit(solution)/shard_map/pallas_call | solution.py:130
  17.5 2.3 %collective-permute-start.2 = (f32[8000,128]{1,0:T(8,128)}, f32[8000,128]{1,0:T(8,128)}, u32[]{:S(2)}, u32[]{:S(2)}) collective-permute-start(f32[8000,128]{1,0:T(8,128)} %shard_map.37), channel_id=1, source_target_pairs={{0,1},{1,0},{2,3},{3,2},{4,5},{5,4},{6,7},{7,6},{8,9},{9,8},{10,11... | collective-permute-start | bytes 12288008 | tf_op jit(solution)/shard_map/ppermute | solution.py:49
  19.8 0.5 collective-permute-start
  20.4 5.2 %collective-permute-done = f32[200,128]{1,0:T(8,128)S(1)} collective-permute-done((f32[200,128]{1,0:T(8,128)S(1)}, f32[200,128]{1,0:T(8,128)S(1)}, u32[]{:S(2)}, u32[]{:S(2)}) %collective-permute-start) | collective-permute-done | bytes 102432 | tf_op jit(solution)/shard_map/ppermute | solution.py:49
  25.7 0.7 copy-done.8
  26.4 7.2 %shard_map.38 = (bf16[640,1600]{1,0:T(8,128)(2,1)}, bf16[640,1600]{1,0:T(8,128)(2,1)}) custom-call(s32[1,160]{1,0:T(1,128)} %get-tuple-element.37.source_ref, f32[640,3200]{1,0:T(8,128)} %left_ref.3), custom_call_target="tpu_custom_call" | custom-call | flops 1310720000 | bytes 12288000 | tf_op jit(solution)/shard_map/pallas_call | solution.py:130
  33.6 24.7 %all-gather.3.cloned.1.call-done = f32[6400,128]{1,0:T(8,128)} async-done(((f32[800,128]{1,0:T(8,128)}), f32[6400,128]{1,0:T(8,128)}) %all-gather.3.cloned.1.call-update) | async-done | bytes 3276816 | tf_op jit(solution)/shard_map/all_gather | solution.py:248
  58.4 2.4 %slice_bitcast_fusion.9 = (f32[8,1,200,128]{3,2,1,0:T(8,128)}, f32[8,200,128]{2,1,0:T(8,128)}) fusion(f32[8,800,128]{2,1,0:T(8,128)} %bitcast.59), kind=kLoop, calls=%fused_computation.50 | loop fusion | bytes 2457600 | tf_op jit(solution)/shard_map/broadcast_in_dim | solution.py:265
  60.8 1.4 collective-permute-start.1
  62.2 2.1 %slice_bitcast_fusion.8 = (f32[8,1,200,128]{3,2,1,0:T(8,128)S(1)}, f32[8,200,128]{2,1,0:T(8,128)}) fusion(f32[8,800,128]{2,1,0:T(8,128)} %bitcast.60), kind=kLoop, calls=%fused_computation.49 | loop fusion | bytes 2457600 | tf_op jit(solution)/shard_map/broadcast_in_dim | solution.py:265
  64.4 0.6 collective-permute-start.3
  65.2 1.4 slice_bitcast_fusion.7
  66.6 1.5 collective-permute-start.5
  68.1 1.3 slice_bitcast_fusion.6
  69.4 0.2 collective-permute-done.2.refs_4_.refs_3_
  69.6 4.4 %collective-permute-done.1.refs_1_ = f32[1600,128]{1,0:T(8,128)} collective-permute-done((f32[1600,128]{1,0:T(8,128)}, f32[1600,128]{1,0:T(8,128)}, u32[]{:S(2)}, u32[]{:S(2)}) %collective-permute-start.1) | collective-permute-done | bytes 819232 | tf_op jit(solution)/shard_map/ppermute | solution.py:49
  74.0 1.1 copy-done.3
  75.1 6.9 %shard_map.39 = (f32[2,2,10,16,256]{4,3,2,1,0:T(8,128)S(1)}, f32[2,2,10,16,256]{4,3,2,1,0:T(8,128)S(1)}) custom-call(s32[9]{0:T(128)S(1)} %pad_add_fusion.1.place_ref, f32[8,1,200,128]{3,2,1,0:T(8,128)S(1)} %copy-done.3, f32[1600,128]{1,0:T(8,128)} %collective-permute-done.1.refs_1_, bf16[640,1600]{1,0:T(8,128)(2,1)S(1)} %copy-done, ...), custom_call_target="tpu_custom_call" | custom-call | flops 163840 | bytes 163840 | tf_op jit(solution)/shard_map/pallas_call | solution.py:202
  82.0 1.8 %collective-permute-start.4 = (f32[2,2,10,16,256]{4,3,2,1,0:T(8,128)S(1)}, f32[2,2,10,16,256]{4,3,2,1,0:T(8,128)S(1)}, u32[]{:S(2)}, u32[]{:S(2)}) collective-permute-start(f32[2,2,10,16,256]{4,3,2,1,0:T(8,128)S(1)} %get-tuple-element.50), channel_id=1, source_target_pairs={{0,64},{1,65},{2,66},{3,67},{4,68},{5,69},{6,70},{7,71},{8,72},{9,... | collective-permute-start | bytes 1966088 | tf_op jit(solution)/shard_map/ppermute | solution.py:49
  83.9 6.8 %shard_map.40 = (f32[2,2,10,16,256]{4,3,2,1,0:T(8,128)S(1)}, f32[2,2,10,16,256]{4,3,2,1,0:T(8,128)S(1)}) custom-call(s32[9]{0:T(128)S(1)} %pad_add_fusion.1.place_ref, f32[8,1,200,128]{3,2,1,0:T(8,128)S(1)} %get-tuple-element.73.refs_0_, f32[1600,128]{1,0:T(8,128)} %collective-permute-done.3.refs_1_, bf16[640,1600]{1,0:T(8,128)(2,1)S(1)} %copy-done, ...), custom_call_target="tpu_custom_call" | custom-call | flops 163840 | bytes 163840 | tf_op jit(solution)/shard_map/pallas_call | solution.py:202
  90.7 0.6 collective-permute-start.6
  91.3 1.5 collective-permute-start.7
  93.0 6.6 %shard_map.41 = (f32[2,2,10,16,256]{4,3,2,1,0:T(8,128)S(1)}, f32[2,2,10,16,256]{4,3,2,1,0:T(8,128)S(1)}) custom-call(s32[9]{0:T(128)S(1)} %pad_add_fusion.1.place_ref, f32[8,1,200,128]{3,2,1,0:T(8,128)S(1)} %get-tuple-element.71.refs_0_, f32[1600,128]{1,0:T(8,128)S(1)} %collective-permute-done.5.refs_1_, bf16[640,1600]{1,0:T(8,128)(2,1)S(1)} %copy-done, ...), custom_call_target="tpu_custom_call" | custom-call | flops 163840 | bytes 163840 | tf_op jit(solution)/shard_map/pallas_call | solution.py:202
  99.6 1.7 %collective-permute-start.8 = (f32[2,2,10,16,256]{4,3,2,1,0:T(8,128)S(1)}, f32[2,2,10,16,256]{4,3,2,1,0:T(8,128)S(1)}, u32[]{:S(2)}, u32[]{:S(2)}) collective-permute-start(f32[2,2,10,16,256]{4,3,2,1,0:T(8,128)S(1)} %get-tuple-element.60), channel_id=1, source_target_pairs={{0,64},{1,65},{2,66},{3,67},{4,68},{5,69},{6,70},{7,71},{8,72},{9,... | collective-permute-start | bytes 1966088 | tf_op jit(solution)/shard_map/ppermute | solution.py:49
  101.4 0.1 add.228
  101.5 2.3 %collective-permute-start.18 = (f32[2,10,16,256]{3,2,1,0:T(8,128)S(1)}, f32[2,10,16,256]{3,2,1,0:T(8,128)S(1)}, u32[]{:S(2)}, u32[]{:S(2)}) collective-permute-start(f32[2,10,16,256]{3,2,1,0:T(8,128)S(1)} %slice_bitcast_fusion.5), channel_id=1, source_target_pairs={{0,192},{1,193},{2,194},{3,195},{4,196},{5,197},{6,198},{7,199},{8... | collective-permute-start | bytes 983048 | tf_op jit(solution)/shard_map/ppermute | solution.py:49
  103.8 7.3 %shard_map.42 = (f32[2,2,10,16,256]{4,3,2,1,0:T(8,128)S(1)}, f32[2,2,10,16,256]{4,3,2,1,0:T(8,128)}) custom-call(s32[9]{0:T(128)S(1)} %pad_add_fusion.1.place_ref, f32[8,1,200,128]{3,2,1,0:T(8,128)S(1)} %get-tuple-element.69.refs_0_, f32[1600,128]{1,0:T(8,128)S(1)} %collective-permute-done.7.refs_1_, bf16[640,1600]{1,0:T(8,128)(2,1)S(1)} %copy-done, ...), custom_call_target="tpu_custom_call" | custom-call | flops 163840 | bytes 163840 | tf_op jit(solution)/shard_map/pallas_call | solution.py:202
  111.2 1.3 collective-permute-start.9
  112.5 0.8 slice_bitcast_fusion.4
  113.3 2.2 %collective-permute-start.19 = (f32[2,10,16,256]{3,2,1,0:T(8,128)}, f32[2,10,16,256]{3,2,1,0:T(8,128)}, u32[]{:S(2)}, u32[]{:S(2)}) collective-permute-start(f32[2,10,16,256]{3,2,1,0:T(8,128)} %slice_bitcast_fusion.4), channel_id=1, source_target_pairs={{0,192},{1,193},{2,194},{3,195},{4,196},{5,197},{6,198},{7,199},{8... | collective-permute-start | bytes 983048 | tf_op jit(solution)/shard_map/ppermute | solution.py:49
  115.5 0.1 add.229
  115.6 0.9 copy-done.5
  116.4 0.7 slice_bitcast_fusion.2
  117.2 1.4 collective-permute-start.20
  118.6 0.8 bitcast_add_fusion.1
  119.3 1.6 copy-done.2
  121.0 1.4 copy-done.4
  122.4 6.7 %shard_map.43 = (f32[2,2,10,16,256]{4,3,2,1,0:T(8,128)S(1)}, f32[2,2,10,16,256]{4,3,2,1,0:T(8,128)S(1)}) custom-call(s32[9]{0:T(128)S(1)} %pad_add_fusion.1.place_ref, f32[3200,128]{1,0:T(8,128)S(1)} %copy-done.4, bf16[640,1600]{1,0:T(8,128)(2,1)S(1)} %copy-done, bf16[640,1600]{1,0:T(8,128)(2,1)S(1)} %copy-done.2, ...), custom_call_target="tpu_custom_call" | custom-call | flops 163840 | bytes 163840 | tf_op jit(solution)/shard_map/pallas_call | solution.py:202
  129.2 0.4 collective-permute-start.10
  129.6 1.2 add.230
  130.8 1.0 bitcast_add_fusion
  131.9 1.0 fusion.7
  133.1 2.6 %collective-permute-start.22 = (f32[10,8,768]{2,1,0:T(8,128)S(1)}, f32[10,8,768]{2,1,0:T(8,128)S(1)}, u32[]{:S(2)}, u32[]{:S(2)}) collective-permute-start(f32[10,8,768]{2,1,0:T(8,128)S(1)} %get-tuple-element.88), channel_id=1, source_target_pairs={{0,1},{1,0},{2,3},{3,2},{4,5},{5,4},{6,7},{7,6},{8,9},{9,8},{10,11... | collective-permute-start | bytes 737288 | tf_op jit(solution)/shard_map/ppermute | solution.py:49
  135.7 0.4 collective-permute-start.23
  136.1 1.9 %collective-permute-start.21 = (f32[10,8,768]{2,1,0:T(8,128)S(1)}, f32[10,8,768]{2,1,0:T(8,128)S(1)}, u32[]{:S(2)}, u32[]{:S(2)}) collective-permute-start(f32[10,8,768]{2,1,0:T(8,128)S(1)} %slice.161), channel_id=1, source_target_pairs={{0,32},{1,33},{2,34},{3,35},{4,36},{5,37},{6,38},{7,39},{8,40},{9,... | collective-permute-start | bytes 737288 | tf_op jit(solution)/shard_map/ppermute | solution.py:49
  138.0 2.0 %collective-permute-done.10 = f32[2,2,10,16,256]{4,3,2,1,0:T(8,128)S(1)} collective-permute-done((f32[2,2,10,16,256]{4,3,2,1,0:T(8,128)S(1)}, f32[2,2,10,16,256]{4,3,2,1,0:T(8,128)S(1)}, u32[]{:S(2)}, u32[]{:S(2)}) %collective-permute-start.10) | collective-permute-done | bytes 655392 | tf_op jit(solution)/shard_map/ppermute | solution.py:49
  140.0 0.1 add.231
  140.2 0.2 fusion.6
  140.4 1.9 %collective-permute-start.11 = (f32[10,8,512]{2,1,0:T(8,128)S(1)}, f32[10,8,512]{2,1,0:T(8,128)S(1)}, u32[]{:S(2)}, u32[]{:S(2)}) collective-permute-start(f32[10,8,512]{2,1,0:T(8,128)S(1)} %get-tuple-element.90), channel_id=1, source_target_pairs={{0,192},{1,193},{2,194},{3,195},{4,196},{5,197},{6,198},{7,199},{8... | collective-permute-start | bytes 491528 | tf_op jit(solution)/shard_map/ppermute | solution.py:49
  142.3 0.1 collective-permute-start.12
  142.5 3.4 %collective-permute-start.13 = (f32[10,8,512]{2,1,0:T(8,128)S(1)}, f32[10,8,512]{2,1,0:T(8,128)S(1)}, u32[]{:S(2)}, u32[]{:S(2)}) collective-permute-start(f32[10,8,512]{2,1,0:T(8,128)S(1)} %get-tuple-element.92), channel_id=1, source_target_pairs={{0,193},{1,192},{2,195},{3,194},{4,197},{5,196},{6,199},{7,198},{8... | collective-permute-start | bytes 491528 | tf_op jit(solution)/shard_map/ppermute | solution.py:49
  146.0 3.6 %collective-permute-start.14 = (f32[10,8,512]{2,1,0:T(8,128)S(1)}, f32[10,8,512]{2,1,0:T(8,128)S(1)}, u32[]{:S(2)}, u32[]{:S(2)}) collective-permute-start(f32[10,8,512]{2,1,0:T(8,128)S(1)} %get-tuple-element.93), channel_id=1, source_target_pairs={{0,225},{1,224},{2,227},{3,226},{4,229},{5,228},{6,231},{7,230},{8... | collective-permute-start | bytes 491528 | tf_op jit(solution)/shard_map/ppermute | solution.py:49
  149.7 0.8 collective-permute-done.12
  150.5 1.9 %collective-permute-done.14 = f32[10,8,512]{2,1,0:T(8,128)S(1)} collective-permute-done((f32[10,8,512]{2,1,0:T(8,128)S(1)}, f32[10,8,512]{2,1,0:T(8,128)S(1)}, u32[]{:S(2)}, u32[]{:S(2)}) %collective-permute-start.14) | collective-permute-done | bytes 163872 | tf_op jit(solution)/shard_map/ppermute | solution.py:49
  152.4 2.5 %collective-permute-done.15 = f32[10,8,512]{2,1,0:T(8,128)S(1)} collective-permute-done((f32[10,8,512]{2,1,0:T(8,128)S(1)}, f32[10,8,512]{2,1,0:T(8,128)S(1)}, u32[]{:S(2)}, u32[]{:S(2)}) %collective-permute-start.15) | collective-permute-done | bytes 163872 | tf_op jit(solution)/shard_map/ppermute | solution.py:49
  154.9 1.0 collective-permute-done.16
  155.9 0.1 fusion.16
  156.1 0.4 reshape.164
  156.5 0.1 reshape.165
  156.6 0.4 copy-done.9
  157.1 0.8 add.245
  (70 shorter events, 1.7 us)
Async XLA Ops:
  6.5 51.8 %all-gather.3.cloned.1.call-start = ((), (), s32[]{:S(2)}) async-start(), calls=%async_computation | async-start | bytes 3686400 | tf_op jit(solution)/shard_map/all_gather | solution.py:248
  8.7 110.6 %all-gather.5.cloned.1.call-start = ((), (), s32[]{:S(2)}) async-start(), calls=%async_computation.1 | async-start | bytes 1843200 | tf_op jit(solution)/shard_map/all_gather | solution.py:250
  17.5 52.1 %collective-permute-start.2 = (f32[8000,128]{1,0:T(8,128)}, f32[8000,128]{1,0:T(8,128)}, u32[]{:S(2)}, u32[]{:S(2)}) collective-permute-start(f32[8000,128]{1,0:T(8,128)} %shard_map.37), channel_id=1, source_target_pairs={{0,1},{1,0},{2,3},{3,2},{4,5},{5,4},{6,7},{7,6},{8,9},{9,8},{10,11... | collective-permute-start | bytes 12288008 | tf_op jit(solution)/shard_map/ppermute | solution.py:49
  19.8 5.9 %collective-permute-start = (f32[200,128]{1,0:T(8,128)S(1)}, f32[200,128]{1,0:T(8,128)S(1)}, u32[]{:S(2)}, u32[]{:S(2)}) collective-permute-start(f32[200,128]{1,0:T(8,128)S(1)} %reshape.159), channel_id=1, source_target_pairs={{0,3},{1,2},{2,1},{3,0},{4,7},{5,6},{6,5},{7,4},{8,11},{9,10},{10,... | collective-permute-start | bytes 307208 | tf_op jit(solution)/shard_map/ppermute | solution.py:49
  25.7 0.7 copy-start.8
  60.8 13.2 %collective-permute-start.1 = (f32[1600,128]{1,0:T(8,128)}, f32[1600,128]{1,0:T(8,128)}, u32[]{:S(2)}, u32[]{:S(2)}) collective-permute-start(f32[1600,128]{1,0:T(8,128)} %bitcast.12), channel_id=1, source_target_pairs={{0,3},{1,2},{2,1},{3,0},{4,7},{5,6},{6,5},{7,4},{8,11},{9,10},{10,... | collective-permute-start | bytes 2457608 | tf_op jit(solution)/shard_map/ppermute | solution.py:49
  64.4 19.5 %collective-permute-start.3 = (f32[1600,128]{1,0:T(8,128)}, f32[1600,128]{1,0:T(8,128)}, u32[]{:S(2)}, u32[]{:S(2)}) collective-permute-start(f32[1600,128]{1,0:T(8,128)} %bitcast.13), channel_id=1, source_target_pairs={{0,3},{1,2},{2,1},{3,0},{4,7},{5,6},{6,5},{7,4},{8,11},{9,10},{10,... | collective-permute-start | bytes 2457608 | tf_op jit(solution)/shard_map/ppermute | solution.py:49
  65.2 8.8 %copy-start = (bf16[640,1600]{1,0:T(8,128)(2,1)S(1)}, bf16[640,1600]{1,0:T(8,128)(2,1)}, u32[]{:S(2)}) copy-start(bf16[640,1600]{1,0:T(8,128)(2,1)} %get-tuple-element.38.refs_2_.refs_1_) | copy-start | bytes 6144004
  65.2 8.8 %copy-start.1 = (bf16[640,1600]{1,0:T(8,128)(2,1)S(1)}, bf16[640,1600]{1,0:T(8,128)(2,1)}, u32[]{:S(2)}) copy-start(bf16[640,1600]{1,0:T(8,128)(2,1)} %get-tuple-element.44.refs_3_.refs_2_) | copy-start | bytes 6144004
  66.6 26.4 %collective-permute-start.5 = (f32[1600,128]{1,0:T(8,128)S(1)}, f32[1600,128]{1,0:T(8,128)S(1)}, u32[]{:S(2)}, u32[]{:S(2)}) collective-permute-start(f32[1600,128]{1,0:T(8,128)S(1)} %bitcast.65), channel_id=1, source_target_pairs={{0,3},{1,2},{2,1},{3,0},{4,7},{5,6},{6,5},{7,4},{8,11},{9,10},{10,... | collective-permute-start | bytes 2457608 | tf_op jit(solution)/shard_map/ppermute | solution.py:49
  74.0 1.1 copy-start.3
  82.0 10.9 %collective-permute-start.4 = (f32[2,2,10,16,256]{4,3,2,1,0:T(8,128)S(1)}, f32[2,2,10,16,256]{4,3,2,1,0:T(8,128)S(1)}, u32[]{:S(2)}, u32[]{:S(2)}) collective-permute-start(f32[2,2,10,16,256]{4,3,2,1,0:T(8,128)S(1)} %get-tuple-element.50), channel_id=1, source_target_pairs={{0,64},{1,65},{2,66},{3,67},{4,68},{5,69},{6,70},{7,71},{8,72},{9,... | collective-permute-start | bytes 1966088 | tf_op jit(solution)/shard_map/ppermute | solution.py:49
  90.7 10.7 %collective-permute-start.6 = (f32[2,2,10,16,256]{4,3,2,1,0:T(8,128)S(1)}, f32[2,2,10,16,256]{4,3,2,1,0:T(8,128)S(1)}, u32[]{:S(2)}, u32[]{:S(2)}) collective-permute-start(f32[2,2,10,16,256]{4,3,2,1,0:T(8,128)S(1)} %get-tuple-element.55), channel_id=1, source_target_pairs={{0,64},{1,65},{2,66},{3,67},{4,68},{5,69},{6,70},{7,71},{8,72},{9,... | collective-permute-start | bytes 1966088 | tf_op jit(solution)/shard_map/ppermute | solution.py:49
  91.3 12.5 %collective-permute-start.7 = (f32[1600,128]{1,0:T(8,128)S(1)}, f32[1600,128]{1,0:T(8,128)S(1)}, u32[]{:S(2)}, u32[]{:S(2)}) collective-permute-start(f32[1600,128]{1,0:T(8,128)S(1)} %bitcast.64), channel_id=1, source_target_pairs={{0,3},{1,2},{2,1},{3,0},{4,7},{5,6},{6,5},{7,4},{8,11},{9,10},{10,... | collective-permute-start | bytes 2457608 | tf_op jit(solution)/shard_map/ppermute | solution.py:49
  99.6 15.8 %collective-permute-start.8 = (f32[2,2,10,16,256]{4,3,2,1,0:T(8,128)S(1)}, f32[2,2,10,16,256]{4,3,2,1,0:T(8,128)S(1)}, u32[]{:S(2)}, u32[]{:S(2)}) collective-permute-start(f32[2,2,10,16,256]{4,3,2,1,0:T(8,128)S(1)} %get-tuple-element.60), channel_id=1, source_target_pairs={{0,64},{1,65},{2,66},{3,67},{4,68},{5,69},{6,70},{7,71},{8,72},{9,... | collective-permute-start | bytes 1966088 | tf_op jit(solution)/shard_map/ppermute | solution.py:49
  101.5 17.0 %collective-permute-start.18 = (f32[2,10,16,256]{3,2,1,0:T(8,128)S(1)}, f32[2,10,16,256]{3,2,1,0:T(8,128)S(1)}, u32[]{:S(2)}, u32[]{:S(2)}) collective-permute-start(f32[2,10,16,256]{3,2,1,0:T(8,128)S(1)} %slice_bitcast_fusion.5), channel_id=1, source_target_pairs={{0,192},{1,193},{2,194},{3,195},{4,196},{5,197},{6,198},{7,199},{8... | collective-permute-start | bytes 983048 | tf_op jit(solution)/shard_map/ppermute | solution.py:49
  111.2 18.4 %collective-permute-start.9 = (f32[2,2,10,16,256]{4,3,2,1,0:T(8,128)}, f32[2,2,10,16,256]{4,3,2,1,0:T(8,128)}, u32[]{:S(2)}, u32[]{:S(2)}) collective-permute-start(f32[2,2,10,16,256]{4,3,2,1,0:T(8,128)} %get-tuple-element.64), channel_id=1, source_target_pairs={{0,64},{1,65},{2,66},{3,67},{4,68},{5,69},{6,70},{7,71},{8,72},{9,... | collective-permute-start | bytes 1966088 | tf_op jit(solution)/shard_map/ppermute | solution.py:49
  113.3 17.5 %collective-permute-start.19 = (f32[2,10,16,256]{3,2,1,0:T(8,128)}, f32[2,10,16,256]{3,2,1,0:T(8,128)}, u32[]{:S(2)}, u32[]{:S(2)}) collective-permute-start(f32[2,10,16,256]{3,2,1,0:T(8,128)} %slice_bitcast_fusion.4), channel_id=1, source_target_pairs={{0,192},{1,193},{2,194},{3,195},{4,196},{5,197},{6,198},{7,199},{8... | collective-permute-start | bytes 983048 | tf_op jit(solution)/shard_map/ppermute | solution.py:49
  115.6 0.9 copy-start.5
  117.2 14.7 %collective-permute-start.20 = (f32[2,10,16,256]{3,2,1,0:T(8,128)}, f32[2,10,16,256]{3,2,1,0:T(8,128)}, u32[]{:S(2)}, u32[]{:S(2)}) collective-permute-start(f32[2,10,16,256]{3,2,1,0:T(8,128)} %slice_bitcast_fusion.2), channel_id=1, source_target_pairs={{0,192},{1,193},{2,194},{3,195},{4,196},{5,197},{6,198},{7,199},{8... | collective-permute-start | bytes 983048 | tf_op jit(solution)/shard_map/ppermute | solution.py:49
  119.3 1.6 copy-start.2
  120.9 1.4 copy-start.4
  129.1 2.7 %copy-start.6 = (f32[2,2,10,16,256]{4,3,2,1,0:T(8,128)S(1)}, f32[2,2,10,16,256]{4,3,2,1,0:T(8,128)}, u32[]{:S(2)}) copy-start(f32[2,2,10,16,256]{4,3,2,1,0:T(8,128)} %copy-done.5) | copy-start | bytes 1966084
  129.1 3.7 %copy-start.7 = (f32[2,10,16,256]{3,2,1,0:T(8,128)S(1)}, f32[2,10,16,256]{3,2,1,0:T(8,128)}, u32[]{:S(2)}) copy-start(f32[2,10,16,256]{3,2,1,0:T(8,128)} %bitcast_add_fusion.1) | copy-start | bytes 983044
  129.2 10.9 %collective-permute-start.10 = (f32[2,2,10,16,256]{4,3,2,1,0:T(8,128)S(1)}, f32[2,2,10,16,256]{4,3,2,1,0:T(8,128)S(1)}, u32[]{:S(2)}, u32[]{:S(2)}) collective-permute-start(f32[2,2,10,16,256]{4,3,2,1,0:T(8,128)S(1)} %get-tuple-element.65), channel_id=1, source_target_pairs={{0,64},{1,65},{2,66},{3,67},{4,68},{5,69},{6,70},{7,71},{8,72},{9,... | collective-permute-start | bytes 1966088 | tf_op jit(solution)/shard_map/ppermute | solution.py:49
  133.1 9.4 %collective-permute-start.22 = (f32[10,8,768]{2,1,0:T(8,128)S(1)}, f32[10,8,768]{2,1,0:T(8,128)S(1)}, u32[]{:S(2)}, u32[]{:S(2)}) collective-permute-start(f32[10,8,768]{2,1,0:T(8,128)S(1)} %get-tuple-element.88), channel_id=1, source_target_pairs={{0,1},{1,0},{2,3},{3,2},{4,5},{5,4},{6,7},{7,6},{8,9},{9,8},{10,11... | collective-permute-start | bytes 737288 | tf_op jit(solution)/shard_map/ppermute | solution.py:49
  135.7 10.3 %collective-permute-start.23 = (f32[10,8,768]{2,1,0:T(8,128)S(1)}, f32[10,8,768]{2,1,0:T(8,128)S(1)}, u32[]{:S(2)}, u32[]{:S(2)}) collective-permute-start(f32[10,8,768]{2,1,0:T(8,128)S(1)} %get-tuple-element.89), channel_id=1, source_target_pairs={{0,33},{1,32},{2,35},{3,34},{4,37},{5,36},{6,39},{7,38},{8,41},{9,... | collective-permute-start | bytes 737288 | tf_op jit(solution)/shard_map/ppermute | solution.py:49
  136.1 13.5 %collective-permute-start.21 = (f32[10,8,768]{2,1,0:T(8,128)S(1)}, f32[10,8,768]{2,1,0:T(8,128)S(1)}, u32[]{:S(2)}, u32[]{:S(2)}) collective-permute-start(f32[10,8,768]{2,1,0:T(8,128)S(1)} %slice.161), channel_id=1, source_target_pairs={{0,32},{1,33},{2,34},{3,35},{4,36},{5,37},{6,38},{7,39},{8,40},{9,... | collective-permute-start | bytes 737288 | tf_op jit(solution)/shard_map/ppermute | solution.py:49
  140.4 9.2 %collective-permute-start.11 = (f32[10,8,512]{2,1,0:T(8,128)S(1)}, f32[10,8,512]{2,1,0:T(8,128)S(1)}, u32[]{:S(2)}, u32[]{:S(2)}) collective-permute-start(f32[10,8,512]{2,1,0:T(8,128)S(1)} %get-tuple-element.90), channel_id=1, source_target_pairs={{0,192},{1,193},{2,194},{3,195},{4,196},{5,197},{6,198},{7,199},{8... | collective-permute-start | bytes 491528 | tf_op jit(solution)/shard_map/ppermute | solution.py:49
  142.3 8.1 %collective-permute-start.12 = (f32[10,8,512]{2,1,0:T(8,128)S(1)}, f32[10,8,512]{2,1,0:T(8,128)S(1)}, u32[]{:S(2)}, u32[]{:S(2)}) collective-permute-start(f32[10,8,512]{2,1,0:T(8,128)S(1)} %get-tuple-element.91), channel_id=1, source_target_pairs={{0,224},{1,225},{2,226},{3,227},{4,228},{5,229},{6,230},{7,231},{8... | collective-permute-start | bytes 491528 | tf_op jit(solution)/shard_map/ppermute | solution.py:49
  142.5 8.0 %collective-permute-start.13 = (f32[10,8,512]{2,1,0:T(8,128)S(1)}, f32[10,8,512]{2,1,0:T(8,128)S(1)}, u32[]{:S(2)}, u32[]{:S(2)}) collective-permute-start(f32[10,8,512]{2,1,0:T(8,128)S(1)} %get-tuple-element.92), channel_id=1, source_target_pairs={{0,193},{1,192},{2,195},{3,194},{4,197},{5,196},{6,199},{7,198},{8... | collective-permute-start | bytes 491528 | tf_op jit(solution)/shard_map/ppermute | solution.py:49
  146.0 6.4 %collective-permute-start.14 = (f32[10,8,512]{2,1,0:T(8,128)S(1)}, f32[10,8,512]{2,1,0:T(8,128)S(1)}, u32[]{:S(2)}, u32[]{:S(2)}) collective-permute-start(f32[10,8,512]{2,1,0:T(8,128)S(1)} %get-tuple-element.93), channel_id=1, source_target_pairs={{0,225},{1,224},{2,227},{3,226},{4,229},{5,228},{6,231},{7,230},{8... | collective-permute-start | bytes 491528 | tf_op jit(solution)/shard_map/ppermute | solution.py:49
  149.6 5.3 %collective-permute-start.15 = (f32[10,8,512]{2,1,0:T(8,128)S(1)}, f32[10,8,512]{2,1,0:T(8,128)S(1)}, u32[]{:S(2)}, u32[]{:S(2)}) collective-permute-start(f32[10,8,512]{2,1,0:T(8,128)S(1)} %get-tuple-element.94), channel_id=1, source_target_pairs={{0,1},{1,0},{2,3},{3,2},{4,5},{5,4},{6,7},{7,6},{8,9},{9,8},{10,11... | collective-permute-start | bytes 491528 | tf_op jit(solution)/shard_map/ppermute | solution.py:49
  149.6 6.3 %collective-permute-start.16 = (f32[10,8,512]{2,1,0:T(8,128)S(1)}, f32[10,8,512]{2,1,0:T(8,128)S(1)}, u32[]{:S(2)}, u32[]{:S(2)}) collective-permute-start(f32[10,8,512]{2,1,0:T(8,128)S(1)} %get-tuple-element.95), channel_id=1, source_target_pairs={{0,33},{1,32},{2,35},{3,34},{4,37},{5,36},{6,39},{7,38},{8,41},{9,... | collective-permute-start | bytes 491528 | tf_op jit(solution)/shard_map/ppermute | solution.py:49
  150.5 5.5 %collective-permute-start.17 = (f32[10,8,512]{2,1,0:T(8,128)S(1)}, f32[10,8,512]{2,1,0:T(8,128)S(1)}, u32[]{:S(2)}, u32[]{:S(2)}) collective-permute-start(f32[10,8,512]{2,1,0:T(8,128)S(1)} %slice.154), channel_id=1, source_target_pairs={{0,32},{1,33},{2,34},{3,35},{4,36},{5,37},{6,38},{7,39},{8,40},{9,... | collective-permute-start | bytes 491528 | tf_op jit(solution)/shard_map/ppermute | solution.py:49
  156.0 1.0 copy-start.9
Sparse Core Ops, SparseCore 0:
  9.1 49.1 all-gather.2
  60.2 38.6 all-gather.4

commit v4 on v3

--- a/solution.py
+++ b/solution.py
@@ -138,8 +138,12 @@
     )(source, left)
 
 
-def product_kernel(k_local, tiles, ringed, place_ref, *refs):
-    *pieces, high_ref, low_ref, got_ref, keep_ref, send_ref, right_high, right_low, total_ref = refs
+def product_kernel(k_local, tiles, ringed, raw, place_ref, *refs):
+    *refs, right_high, right_low, total_ref = refs
+    if raw:
+        *pieces, high_ref, low_ref, got_ref, keep_ref, send_ref, got_high_ref, got_low_ref = refs
+    else:
+        *pieces, high_ref, low_ref, got_high_ref, got_low_ref, keep_ref, send_ref = refs
     shared = Z * O // 8
     size = O // 8 * k_local * tiles
 
@@ -169,24 +173,32 @@
 
     rows, depth = high_ref.shape
     full = depth // LANES
-    got = []
-    for at in range(0, rows * depth // LANES, ARRANGE * depth // LANES):
-        blocks = [got_ref[at + t * ARRANGE : at + (t + 1) * ARRANGE, :] for t in range(full)]
-        rest = got_ref[at + full * ARRANGE : at + ARRANGE * depth // LANES, :]
-        blocks.append(jnp.concatenate([rest[:, : LANES // 2], rest[:, LANES // 2 :]], axis=0))
-        got.append(jnp.concatenate(blocks, axis=1))
-    got_high, got_low = split(jnp.concatenate(got, axis=0))
-    for at, (high, low) in enumerate(((high_ref[...], low_ref[...]), (got_high, got_low))):
-        total_ref[...] = dot(high, right_high[...]) + dot(high, right_low[...]) + dot(low, right_high[...])
+    if raw:
+        got = []
+        for at in range(0, rows * depth // LANES, ARRANGE * depth // LANES):
+            blocks = [got_ref[at + t * ARRANGE : at + (t + 1) * ARRANGE, :] for t in range(full)]
+            rest = got_ref[at + full * ARRANGE : at + ARRANGE * depth // LANES, :]
+            blocks.append(jnp.concatenate([rest[:, : LANES // 2], rest[:, LANES // 2 :]], axis=0))
+            got.append(jnp.concatenate(blocks, axis=1))
+        got_high, got_low = split(jnp.concatenate(got, axis=0))
+        got_high_ref[...] = got_high
+        got_low_ref[...] = got_low
+    else:
+        got_high, got_low = got_high_ref[...], got_low_ref[...]
+    high = jnp.concatenate([high_ref[...], got_high], axis=0)
+    low = jnp.concatenate([low_ref[...], got_low], axis=0)
+    total_ref[...] = dot(high, right_high[...]) + dot(high, right_low[...]) + dot(low, right_high[...])
+    for at in range(2):
         for b in range(rows // NJ):
             for out, slots in ((keep_ref, (0, 1)), (send_ref, (2, 3))):
                 for slot, which in enumerate(slots):
                     for part in range(CORES):
-                        start = pl.multiple_of(b * NJ + place_ref[which * CORES + part] * 8, 8)
+                        start = pl.multiple_of(at * rows + b * NJ + place_ref[which * CORES + part] * 8, 8)
                         out[slot, at, b, part * 8 : (part + 1) * 8, :] = total_ref[pl.ds(start, 8), :]
 
 
 def product(pieces, at, high, low, got, place, k_local, tiles):
+    raw = len(got) == 1
     rows, depth = high.shape
     width = tiles * LANES
     block = BLOCK
@@ -200,24 +212,24 @@
     out = pl.BlockSpec((2, 2, block // NJ, 16, width), lambda m, s: (0, 0, m, 0, 0))
     shape = jax.ShapeDtypeStruct((2, 2, b_local, 16, width), jnp.float32)
     return pl.pallas_call(
-        functools.partial(product_kernel, k_local, tiles, ringed),
+        functools.partial(product_kernel, k_local, tiles, ringed, raw),
         grid_spec=pltpu.PrefetchScalarGridSpec(
             num_scalar_prefetch=1,
             grid=(rows // block,),
-            in_specs=specs + [left, left, away],
-            out_specs=[out, out],
+            in_specs=specs + [left, left] + ([away] if raw else [left, left]),
+            out_specs=[out, out] + ([left, left] if raw else []),
             scratch_shapes=[
                 pltpu.VMEM((depth, width), jnp.bfloat16),
                 pltpu.VMEM((depth, width), jnp.bfloat16),
-                pltpu.VMEM((block, width), jnp.float32),
+                pltpu.VMEM((2 * block, width), jnp.float32),
             ],
         ),
-        out_shape=[shape, shape],
-        compiler_params=pltpu.CompilerParams(vmem_limit_bytes=LIMIT2 * 1024 * 1024),
+        out_shape=[shape, shape] + ([jax.ShapeDtypeStruct(high.shape, high.dtype)] * 2 if raw else []),
+        compiler_params=pltpu.CompilerParams(vmem_limit_bytes=(LIMIT2 if ringed else LIMIT1) * 1024 * 1024),
         cost_estimate=pl.CostEstimate(
             flops=rows * width, bytes_accessed=rows * width, transcendentals=0
         ),
-    )(place, *pieces, high, low, got)
+    )(place, *pieces, high, low, *got)
 
 
 def per_device(amplitudes, integral, residual_in):
@@ -251,7 +263,7 @@
     half = V // 2
     packed = (ARRANGE * k_local * half // LANES, LANES)
     (away,) = arrange(away_kernel, integral, source[:, half:], k_local, [packed], jnp.float32)
-    got = send(away, to_x_mate)
+    got = [send(away, to_x_mate)]
     natural = (ARRANGE, k_local * half)
     high, low = arrange(keep_kernel, integral, after(source[:, :half], away, pair), k_local, [natural] * 2, jnp.bfloat16)
     gathered = after(gathered, high)
@@ -273,7 +285,8 @@
         if n < count:
             if n >= 2:
                 place = after(place, firsts[n - 2])
-            keep, give = product(pieces[n], 0, high, low, got, place, k_local, plan[n])
+            keep, give, *parts = product(pieces[n], 0, high, low, got, place, k_local, plan[n])
+            got = parts or got
             place = after(place, keep)
             keeps.append(keep)
             gives.append(send(give, to_y_mate))

time: 168 us -> 166 us (0.988)
  local copies, waits for them, and re-layouts: 17.8 us -> 12.1 us
  waiting for transfers between devices: 43 us -> 47.1 us
  starting transfers between devices: 33.7 us -> 36.9 us
  other arithmetic: 7 us -> 5.16 us
    ppermute x24, waiting for transfers between devices: 18.2 us -> 22.3 us  [send(): return lax.ppermute(value, ('row', 'col'), links(target))]
    unnamed x21 -> x19, local copies, waits for them, and re-layouts: 6.15 us -> 2.28 us
    ppermute x24, starting transfers between devices: 33.7 us -> 36.9 us  [send(): return lax.ppermute(value, ('row', 'col'), links(target))]
  transfers between devices with their start and end apart: 26 -> 26, of which waited for: 11 -> 11; matrix products, arithmetic and copies ran while one was open for 9% -> 7% of each run, Pallas kernels for 30% -> 29%
where the time goes in v4:
time: 166 us; the launch traced here: 163 us
  Pallas kernels  47.8 us (29%)
  waiting for transfers between devices  47.1 us (28%)
  starting transfers between devices  36.9 us (22%)
  between operations  13.9 us (8%)
  local copies, waits for them, and re-layouts  12.1 us (7%)
  other arithmetic  5.16 us (3%)
    ppermute x24, starting transfers between devices, send(): return lax.ppermute(value, ('row', 'col'), links(target))  36.9 us
    pallas_call x5, Pallas kernels, product(): pl.pallas_call(functools.partial(product_kernel, k_local, tiles, ringed,...  33 us
    all_gather x1, waiting for transfers between devices, per_device(): gathered = gather(jnp.concatenate(rest)).reshape(Z, -1, LANES)  24.7 us
    ppermute x24, waiting for transfers between devices, send(): return lax.ppermute(value, ('row', 'col'), links(target))  22.3 us
    pallas_call x2, Pallas kernels, arrange(): pl.pallas_call(functools.partial(kernel, k_local), grid=(rows // block,),...  14.7 us
    broadcast_in_dim x4, local copies, waits for them, and re-layouts, per_device(): pieces.append([own[:, None], send(outgoing, to_x_other)])  6.04 us
  transfers between devices with their start and end apart: 26, of which 11 were waited for; matrix products, arithmetic and copies ran while one was open for 7% of the time, Pallas kernels for 29%

profile of v4, /device:TPU:2, one launch (start us, length us, event | category | flops | bytes accessed | tf_op | source)
XLA Modules:
  0.0 162.9 jit_solution(926589116616646790)
XLA Ops:
  6.5 1.3 reshape.153
  7.9 0.8 pad_maximum_fusion.2
  9.1 0.1 add.226
  9.3 0.7 fusion.22
  9.9 7.5 %shard_map.37 = f32[8000,128]{1,0:T(8,128)} custom-call(s32[1,160]{1,0:T(1,128)} %get-tuple-element.100.source_ref, f32[640,3200]{1,0:T(8,128)} %left_ref.3), custom_call_target="tpu_custom_call" | custom-call | flops 1310720000 | bytes 12288000 | tf_op jit(solution)/shard_map/pallas_call | solution.py:130
  17.4 2.3 %collective-permute-start.2 = (f32[8000,128]{1,0:T(8,128)}, f32[8000,128]{1,0:T(8,128)}, u32[]{:S(2)}, u32[]{:S(2)}) collective-permute-start(f32[8000,128]{1,0:T(8,128)} %shard_map.37), channel_id=1, source_target_pairs={{0,1},{1,0},{2,3},{3,2},{4,5},{5,4},{6,7},{7,6},{8,9},{9,8},{10,11... | collective-permute-start | bytes 12288008 | tf_op jit(solution)/shard_map/ppermute | solution.py:49
  19.7 0.5 collective-permute-start
  20.4 5.2 %collective-permute-done = f32[200,128]{1,0:T(8,128)S(1)} collective-permute-done((f32[200,128]{1,0:T(8,128)S(1)}, f32[200,128]{1,0:T(8,128)S(1)}, u32[]{:S(2)}, u32[]{:S(2)}) %collective-permute-start) | collective-permute-done | bytes 102432 | tf_op jit(solution)/shard_map/ppermute | solution.py:49
  25.6 0.7 copy-done.7
  26.4 7.2 %shard_map.38 = (bf16[640,1600]{1,0:T(8,128)(2,1)}, bf16[640,1600]{1,0:T(8,128)(2,1)}) custom-call(s32[1,160]{1,0:T(1,128)} %get-tuple-element.39.source_ref, f32[640,3200]{1,0:T(8,128)} %left_ref.3), custom_call_target="tpu_custom_call" | custom-call | flops 1310720000 | bytes 12288000 | tf_op jit(solution)/shard_map/pallas_call | solution.py:130
  33.6 24.7 %all-gather.3.cloned.1.call-done = f32[6400,128]{1,0:T(8,128)} async-done(((f32[800,128]{1,0:T(8,128)}), f32[6400,128]{1,0:T(8,128)}) %all-gather.3.cloned.1.call-update) | async-done | bytes 3276816 | tf_op jit(solution)/shard_map/all_gather | solution.py:260
  58.3 2.1 %slice_bitcast_fusion.9 = (f32[8,1,200,128]{3,2,1,0:T(8,128)}, f32[8,200,128]{2,1,0:T(8,128)S(1)}) fusion(f32[8,800,128]{2,1,0:T(8,128)} %bitcast.59), kind=kLoop, calls=%fused_computation.50 | loop fusion | bytes 2457600 | tf_op jit(solution)/shard_map/broadcast_in_dim | solution.py:277
  60.5 1.5 collective-permute-start.1
  61.9 1.3 slice_bitcast_fusion.8
  63.2 0.6 collective-permute-start.3
  63.9 0.1 add.207
  64.1 1.4 slice_bitcast_fusion.7
  65.5 1.6 collective-permute-start.5
  67.0 1.3 slice_bitcast_fusion.6
  68.3 1.6 collective-permute-done.2.refs_4_
  69.9 4.0 %collective-permute-done.1.refs_1_ = f32[1600,128]{1,0:T(8,128)} collective-permute-done((f32[1600,128]{1,0:T(8,128)S(1)}, f32[1600,128]{1,0:T(8,128)}, u32[]{:S(2)}, u32[]{:S(2)}) %collective-permute-start.1) | collective-permute-done | bytes 819232 | tf_op jit(solution)/shard_map/ppermute | solution.py:49
  74.0 1.1 copy-done.4
  75.1 6.9 %shard_map.39 = (f32[2,2,10,16,256]{4,3,2,1,0:T(8,128)S(1)}, f32[2,2,10,16,256]{4,3,2,1,0:T(8,128)S(1)}, bf16[640,1600]{1,0:T(8,128)(2,1)S(1)}, bf16[640,1600]{1,0:T(8,128)(2,1)S(1)}) custom-call(s32[9]{0:T(128)S(1)} %pad_add_fusion.1.place_ref, f32[8,1,200,128]{3,2,1,0:T(8,128)S(1)} %copy-done.4, f32[1600,128]{1,0:T(8,128)} %collective-permute-done.1.refs_1_, ...), custom_call_target="tpu_custom_call" | custom-call | flops 163840 | bytes 163840 | tf_op jit(solution)/shard_map/pallas_call | solution.py:214
  82.0 1.8 %collective-permute-start.4 = (f32[2,2,10,16,256]{4,3,2,1,0:T(8,128)S(1)}, f32[2,2,10,16,256]{4,3,2,1,0:T(8,128)S(1)}, u32[]{:S(2)}, u32[]{:S(2)}) collective-permute-start(f32[2,2,10,16,256]{4,3,2,1,0:T(8,128)S(1)} %get-tuple-element.54), channel_id=1, source_target_pairs={{0,64},{1,65},{2,66},{3,67},{4,68},{5,69},{6,70},{7,71},{8,72},{9,... | collective-permute-start | bytes 1966088 | tf_op jit(solution)/shard_map/ppermute | solution.py:49
  83.9 6.1 %shard_map.40 = (f32[2,2,10,16,256]{4,3,2,1,0:T(8,128)S(1)}, f32[2,2,10,16,256]{4,3,2,1,0:T(8,128)S(1)}) custom-call(s32[9]{0:T(128)S(1)} %pad_add_fusion.1.place_ref, f32[8,1,200,128]{3,2,1,0:T(8,128)S(1)} %get-tuple-element.77.refs_0_, f32[1600,128]{1,0:T(8,128)} %collective-permute-done.3.refs_1_, bf16[640,1600]{1,0:T(8,128)(2,1)S(1)} %copy-done, ...), custom_call_target="tpu_custom_call" | custom-call | flops 163840 | bytes 163840 | tf_op jit(solution)/shard_map/pallas_call | solution.py:214
  90.0 0.7 collective-permute-start.6
  90.8 1.5 collective-permute-start.7
  92.2 0.7 collective-permute-done.4
  92.9 0.1 add.227
  93.0 5.0 %shard_map.41 = (f32[2,2,10,16,256]{4,3,2,1,0:T(8,128)S(1)}, f32[2,2,10,16,256]{4,3,2,1,0:T(8,128)S(1)}) custom-call(s32[9]{0:T(128)S(1)} %pad_add_fusion.1.place_ref, f32[8,1,200,128]{3,2,1,0:T(8,128)S(1)} %get-tuple-element.75.refs_0_, f32[1600,128]{1,0:T(8,128)S(1)} %collective-permute-done.5.refs_1_, bf16[640,1600]{1,0:T(8,128)(2,1)S(1)} %copy-done, ...), custom_call_target="tpu_custom_call" | custom-call | flops 163840 | bytes 163840 | tf_op jit(solution)/shard_map/pallas_call | solution.py:214
  98.0 1.7 %collective-permute-start.8 = (f32[2,2,10,16,256]{4,3,2,1,0:T(8,128)S(1)}, f32[2,2,10,16,256]{4,3,2,1,0:T(8,128)S(1)}, u32[]{:S(2)}, u32[]{:S(2)}) collective-permute-start(f32[2,2,10,16,256]{4,3,2,1,0:T(8,128)S(1)} %get-tuple-element.64), channel_id=1, source_target_pairs={{0,64},{1,65},{2,66},{3,67},{4,68},{5,69},{6,70},{7,71},{8,72},{9,... | collective-permute-start | bytes 1966088 | tf_op jit(solution)/shard_map/ppermute | solution.py:49
  99.7 1.0 collective-permute-done.6
  100.7 0.1 add.228
  100.9 2.3 %collective-permute-start.18 = (f32[2,10,16,256]{3,2,1,0:T(8,128)S(1)}, f32[2,10,16,256]{3,2,1,0:T(8,128)S(1)}, u32[]{:S(2)}, u32[]{:S(2)}) collective-permute-start(f32[2,10,16,256]{3,2,1,0:T(8,128)S(1)} %slice_bitcast_fusion.5), channel_id=1, source_target_pairs={{0,192},{1,193},{2,194},{3,195},{4,196},{5,197},{6,198},{7,199},{8... | collective-permute-start | bytes 983048 | tf_op jit(solution)/shard_map/ppermute | solution.py:49
  103.2 5.7 %shard_map.42 = (f32[2,2,10,16,256]{4,3,2,1,0:T(8,128)S(1)}, f32[2,2,10,16,256]{4,3,2,1,0:T(8,128)}) custom-call(s32[9]{0:T(128)S(1)} %pad_add_fusion.1.place_ref, f32[8,1,200,128]{3,2,1,0:T(8,128)S(1)} %get-tuple-element.73.refs_0_, f32[1600,128]{1,0:T(8,128)S(1)} %collective-permute-done.7.refs_1_, bf16[640,1600]{1,0:T(8,128)(2,1)S(1)} %copy-done, ...), custom_call_target="tpu_custom_call" | custom-call | flops 163840 | bytes 163840 | tf_op jit(solution)/shard_map/pallas_call | solution.py:214
  108.9 1.3 collective-permute-start.9
  110.2 2.3 %collective-permute-start.19 = (f32[2,10,16,256]{3,2,1,0:T(8,128)S(1)}, f32[2,10,16,256]{3,2,1,0:T(8,128)}, u32[]{:S(2)}, u32[]{:S(2)}) collective-permute-start(f32[2,10,16,256]{3,2,1,0:T(8,128)S(1)} %slice_bitcast_fusion.4), channel_id=1, source_target_pairs={{0,192},{1,193},{2,194},{3,195},{4,196},{5,197},{6,198},{7,199},{8... | collective-permute-start | bytes 983048 | tf_op jit(solution)/shard_map/ppermute | solution.py:49
  112.5 0.1 add.229
  112.6 0.7 slice_bitcast_fusion.2
  113.4 2.7 %collective-permute-start.20 = (f32[2,10,16,256]{3,2,1,0:T(8,128)}, f32[2,10,16,256]{3,2,1,0:T(8,128)}, u32[]{:S(2)}, u32[]{:S(2)}) collective-permute-start(f32[2,10,16,256]{3,2,1,0:T(8,128)} %slice_bitcast_fusion.2), channel_id=1, source_target_pairs={{0,192},{1,193},{2,194},{3,195},{4,196},{5,197},{6,198},{7,199},{8... | collective-permute-start | bytes 983048 | tf_op jit(solution)/shard_map/ppermute | solution.py:49
  116.2 9.3 %shard_map.43 = (f32[2,2,10,16,256]{4,3,2,1,0:T(8,128)}, f32[2,2,10,16,256]{4,3,2,1,0:T(8,128)}) custom-call(s32[9]{0:T(128)} %copy-done.5, f32[3200,128]{1,0:T(8,128)} %all-gather.5.cloned.1.call-done.refs_0_, bf16[640,1600]{1,0:T(8,128)(2,1)} %get-tuple-element.40.refs_2_.refs_1_, bf16[640,1600]{1,0:T(8,128)(2,1)} %get-tuple-element.46.refs_3_.refs_2_, ...), custom_call_target="tpu_custom_call" | custom-call | flops 163840 | bytes 163840 | tf_op jit(solution)/shard_map/pallas_call | solution.py:214
  125.5 0.1 collective-permute-start.10
  125.6 0.1 add.230
  125.7 1.0 bitcast_add_fusion
  126.8 1.8 %collective-permute-done.20 = f32[2,10,16,256]{3,2,1,0:T(8,128)} collective-permute-done((f32[2,10,16,256]{3,2,1,0:T(8,128)}, f32[2,10,16,256]{3,2,1,0:T(8,128)}, u32[]{:S(2)}, u32[]{:S(2)}) %collective-permute-start.20) | collective-permute-done | bytes 327712 | tf_op jit(solution)/shard_map/ppermute | solution.py:49
  128.6 1.0 fusion.7
  129.8 2.3 %collective-permute-start.22 = (f32[10,8,768]{2,1,0:T(8,128)S(1)}, f32[10,8,768]{2,1,0:T(8,128)S(1)}, u32[]{:S(2)}, u32[]{:S(2)}) collective-permute-start(f32[10,8,768]{2,1,0:T(8,128)S(1)} %get-tuple-element.92), channel_id=1, source_target_pairs={{0,1},{1,0},{2,3},{3,2},{4,5},{5,4},{6,7},{7,6},{8,9},{9,8},{10,11... | collective-permute-start | bytes 737288 | tf_op jit(solution)/shard_map/ppermute | solution.py:49
  132.1 2.1 %collective-permute-start.21 = (f32[10,8,768]{2,1,0:T(8,128)S(1)}, f32[10,8,768]{2,1,0:T(8,128)S(1)}, u32[]{:S(2)}, u32[]{:S(2)}) collective-permute-start(f32[10,8,768]{2,1,0:T(8,128)S(1)} %slice.161), channel_id=1, source_target_pairs={{0,32},{1,33},{2,34},{3,35},{4,36},{5,37},{6,38},{7,39},{8,40},{9,... | collective-permute-start | bytes 737288 | tf_op jit(solution)/shard_map/ppermute | solution.py:49
  134.2 2.1 %collective-permute-done.10 = f32[2,2,10,16,256]{4,3,2,1,0:T(8,128)S(1)} collective-permute-done((f32[2,2,10,16,256]{4,3,2,1,0:T(8,128)}, f32[2,2,10,16,256]{4,3,2,1,0:T(8,128)S(1)}, u32[]{:S(2)}, u32[]{:S(2)}) %collective-permute-start.10) | collective-permute-done | bytes 655392 | tf_op jit(solution)/shard_map/ppermute | solution.py:49
  136.3 0.1 add.231
  136.4 0.2 fusion.6
  136.6 0.6 collective-permute-start.11
  137.2 1.5 collective-permute-start.12
  138.8 3.2 %collective-permute-start.13 = (f32[10,8,512]{2,1,0:T(8,128)S(1)}, f32[10,8,512]{2,1,0:T(8,128)S(1)}, u32[]{:S(2)}, u32[]{:S(2)}) collective-permute-start(f32[10,8,512]{2,1,0:T(8,128)S(1)} %get-tuple-element.96), channel_id=1, source_target_pairs={{0,193},{1,192},{2,195},{3,194},{4,197},{5,196},{6,199},{7,198},{8... | collective-permute-start | bytes 491528 | tf_op jit(solution)/shard_map/ppermute | solution.py:49
  141.9 5.9 %collective-permute-start.14 = (f32[10,8,512]{2,1,0:T(8,128)S(1)}, f32[10,8,512]{2,1,0:T(8,128)S(1)}, u32[]{:S(2)}, u32[]{:S(2)}) collective-permute-start(f32[10,8,512]{2,1,0:T(8,128)S(1)} %get-tuple-element.97), channel_id=1, source_target_pairs={{0,225},{1,224},{2,227},{3,226},{4,229},{5,228},{6,231},{7,230},{8... | collective-permute-start | bytes 491528 | tf_op jit(solution)/shard_map/ppermute | solution.py:49
  147.9 0.4 collective-permute-start.17
  148.4 2.3 %collective-permute-done.14 = f32[10,8,512]{2,1,0:T(8,128)S(1)} collective-permute-done((f32[10,8,512]{2,1,0:T(8,128)S(1)}, f32[10,8,512]{2,1,0:T(8,128)S(1)}, u32[]{:S(2)}, u32[]{:S(2)}) %collective-permute-start.14) | collective-permute-done | bytes 163872 | tf_op jit(solution)/shard_map/ppermute | solution.py:49
  150.7 2.5 %collective-permute-done.15 = f32[10,8,512]{2,1,0:T(8,128)S(1)} collective-permute-done((f32[10,8,512]{2,1,0:T(8,128)S(1)}, f32[10,8,512]{2,1,0:T(8,128)S(1)}, u32[]{:S(2)}, u32[]{:S(2)}) %collective-permute-start.15) | collective-permute-done | bytes 163872 | tf_op jit(solution)/shard_map/ppermute | solution.py:49
  153.1 1.0 collective-permute-done.16
  154.2 0.1 fusion.16
  154.4 0.4 reshape.164
  154.7 0.1 reshape.165
  154.9 0.4 copy-done.8
  155.3 0.8 add.245
  (68 shorter events, 1.4 us)
Async XLA Ops:
  6.5 51.8 %all-gather.3.cloned.1.call-start = ((), (), s32[]{:S(2)}) async-start(), calls=%async_computation | async-start | bytes 3686400 | tf_op jit(solution)/shard_map/all_gather | solution.py:260
  8.7 107.4 %all-gather.5.cloned.1.call-start = ((), (), s32[]{:S(2)}) async-start(), calls=%async_computation.1 | async-start | bytes 1843200 | tf_op jit(solution)/shard_map/all_gather | solution.py:262
  17.4 52.5 %collective-permute-start.2 = (f32[8000,128]{1,0:T(8,128)}, f32[8000,128]{1,0:T(8,128)}, u32[]{:S(2)}, u32[]{:S(2)}) collective-permute-start(f32[8000,128]{1,0:T(8,128)} %shard_map.37), channel_id=1, source_target_pairs={{0,1},{1,0},{2,3},{3,2},{4,5},{5,4},{6,7},{7,6},{8,9},{9,8},{10,11... | collective-permute-start | bytes 12288008 | tf_op jit(solution)/shard_map/ppermute | solution.py:49
  19.7 5.9 %collective-permute-start = (f32[200,128]{1,0:T(8,128)S(1)}, f32[200,128]{1,0:T(8,128)S(1)}, u32[]{:S(2)}, u32[]{:S(2)}) collective-permute-start(f32[200,128]{1,0:T(8,128)S(1)} %reshape.159), channel_id=1, source_target_pairs={{0,3},{1,2},{2,1},{3,0},{4,7},{5,6},{6,5},{7,4},{8,11},{9,10},{10,... | collective-permute-start | bytes 307208 | tf_op jit(solution)/shard_map/ppermute | solution.py:49
  25.6 0.7 copy-start.7
  60.5 13.5 %collective-permute-start.1 = (f32[1600,128]{1,0:T(8,128)S(1)}, f32[1600,128]{1,0:T(8,128)}, u32[]{:S(2)}, u32[]{:S(2)}) collective-permute-start(f32[1600,128]{1,0:T(8,128)S(1)} %bitcast.67), channel_id=1, source_target_pairs={{0,3},{1,2},{2,1},{3,0},{4,7},{5,6},{6,5},{7,4},{8,11},{9,10},{10,... | collective-permute-start | bytes 2457608 | tf_op jit(solution)/shard_map/ppermute | solution.py:49
  63.2 20.7 %collective-permute-start.3 = (f32[1600,128]{1,0:T(8,128)S(1)}, f32[1600,128]{1,0:T(8,128)}, u32[]{:S(2)}, u32[]{:S(2)}) collective-permute-start(f32[1600,128]{1,0:T(8,128)S(1)} %bitcast.65), channel_id=1, source_target_pairs={{0,3},{1,2},{2,1},{3,0},{4,7},{5,6},{6,5},{7,4},{8,11},{9,10},{10,... | collective-permute-start | bytes 2457608 | tf_op jit(solution)/shard_map/ppermute | solution.py:49
  64.1 39.1 %copy-start.5 = (s32[9]{0:T(128)}, s32[9]{0:T(128)S(1)}, u32[]{:S(2)}) copy-start(s32[9]{0:T(128)S(1)} %pad_add_fusion.1.place_ref) | copy-start | bytes 112
  64.1 9.9 %copy-start = (bf16[640,1600]{1,0:T(8,128)(2,1)S(1)}, bf16[640,1600]{1,0:T(8,128)(2,1)}, u32[]{:S(2)}) copy-start(bf16[640,1600]{1,0:T(8,128)(2,1)} %get-tuple-element.40.refs_2_.refs_1_) | copy-start | bytes 6144004
  64.1 9.9 %copy-start.1 = (bf16[640,1600]{1,0:T(8,128)(2,1)S(1)}, bf16[640,1600]{1,0:T(8,128)(2,1)}, u32[]{:S(2)}) copy-start(bf16[640,1600]{1,0:T(8,128)(2,1)} %get-tuple-element.46.refs_3_.refs_2_) | copy-start | bytes 6144004
  65.5 27.5 %collective-permute-start.5 = (f32[1600,128]{1,0:T(8,128)S(1)}, f32[1600,128]{1,0:T(8,128)S(1)}, u32[]{:S(2)}, u32[]{:S(2)}) collective-permute-start(f32[1600,128]{1,0:T(8,128)S(1)} %bitcast.66), channel_id=1, source_target_pairs={{0,3},{1,2},{2,1},{3,0},{4,7},{5,6},{6,5},{7,4},{8,11},{9,10},{10,... | collective-permute-start | bytes 2457608 | tf_op jit(solution)/shard_map/ppermute | solution.py:49
  74.0 1.1 copy-start.4
  82.0 21.1 %copy-start.2 = (bf16[640,1600]{1,0:T(8,128)(2,1)}, bf16[640,1600]{1,0:T(8,128)(2,1)S(1)}, u32[]{:S(2)}) copy-start(bf16[640,1600]{1,0:T(8,128)(2,1)S(1)} %get-tuple-element.49.refs_4_.refs_3_) | copy-start | bytes 6144004
  82.0 21.1 %copy-start.3 = (bf16[640,1600]{1,0:T(8,128)(2,1)}, bf16[640,1600]{1,0:T(8,128)(2,1)S(1)}, u32[]{:S(2)}) copy-start(bf16[640,1600]{1,0:T(8,128)(2,1)S(1)} %get-tuple-element.50.refs_5_.refs_4_) | copy-start | bytes 6144004
  82.0 10.9 %collective-permute-start.4 = (f32[2,2,10,16,256]{4,3,2,1,0:T(8,128)S(1)}, f32[2,2,10,16,256]{4,3,2,1,0:T(8,128)S(1)}, u32[]{:S(2)}, u32[]{:S(2)}) collective-permute-start(f32[2,2,10,16,256]{4,3,2,1,0:T(8,128)S(1)} %get-tuple-element.54), channel_id=1, source_target_pairs={{0,64},{1,65},{2,66},{3,67},{4,68},{5,69},{6,70},{7,71},{8,72},{9,... | collective-permute-start | bytes 1966088 | tf_op jit(solution)/shard_map/ppermute | solution.py:49
  90.0 10.7 %collective-permute-start.6 = (f32[2,2,10,16,256]{4,3,2,1,0:T(8,128)S(1)}, f32[2,2,10,16,256]{4,3,2,1,0:T(8,128)S(1)}, u32[]{:S(2)}, u32[]{:S(2)}) collective-permute-start(f32[2,2,10,16,256]{4,3,2,1,0:T(8,128)S(1)} %get-tuple-element.59), channel_id=1, source_target_pairs={{0,64},{1,65},{2,66},{3,67},{4,68},{5,69},{6,70},{7,71},{8,72},{9,... | collective-permute-start | bytes 1966088 | tf_op jit(solution)/shard_map/ppermute | solution.py:49
  90.8 12.4 %collective-permute-start.7 = (f32[1600,128]{1,0:T(8,128)S(1)}, f32[1600,128]{1,0:T(8,128)S(1)}, u32[]{:S(2)}, u32[]{:S(2)}) collective-permute-start(f32[1600,128]{1,0:T(8,128)S(1)} %bitcast.64), channel_id=1, source_target_pairs={{0,3},{1,2},{2,1},{3,0},{4,7},{5,6},{6,5},{7,4},{8,11},{9,10},{10,... | collective-permute-start | bytes 2457608 | tf_op jit(solution)/shard_map/ppermute | solution.py:49
  98.0 14.5 %collective-permute-start.8 = (f32[2,2,10,16,256]{4,3,2,1,0:T(8,128)S(1)}, f32[2,2,10,16,256]{4,3,2,1,0:T(8,128)S(1)}, u32[]{:S(2)}, u32[]{:S(2)}) collective-permute-start(f32[2,2,10,16,256]{4,3,2,1,0:T(8,128)S(1)} %get-tuple-element.64), channel_id=1, source_target_pairs={{0,64},{1,65},{2,66},{3,67},{4,68},{5,69},{6,70},{7,71},{8,72},{9,... | collective-permute-start | bytes 1966088 | tf_op jit(solution)/shard_map/ppermute | solution.py:49
  100.9 15.2 %collective-permute-start.18 = (f32[2,10,16,256]{3,2,1,0:T(8,128)S(1)}, f32[2,10,16,256]{3,2,1,0:T(8,128)S(1)}, u32[]{:S(2)}, u32[]{:S(2)}) collective-permute-start(f32[2,10,16,256]{3,2,1,0:T(8,128)S(1)} %slice_bitcast_fusion.5), channel_id=1, source_target_pairs={{0,192},{1,193},{2,194},{3,195},{4,196},{5,197},{6,198},{7,199},{8... | collective-permute-start | bytes 983048 | tf_op jit(solution)/shard_map/ppermute | solution.py:49
  108.9 16.7 %collective-permute-start.9 = (f32[2,2,10,16,256]{4,3,2,1,0:T(8,128)}, f32[2,2,10,16,256]{4,3,2,1,0:T(8,128)S(1)}, u32[]{:S(2)}, u32[]{:S(2)}) collective-permute-start(f32[2,2,10,16,256]{4,3,2,1,0:T(8,128)} %get-tuple-element.68), channel_id=1, source_target_pairs={{0,64},{1,65},{2,66},{3,67},{4,68},{5,69},{6,70},{7,71},{8,72},{9,... | collective-permute-start | bytes 1966088 | tf_op jit(solution)/shard_map/ppermute | solution.py:49
  110.2 15.5 %collective-permute-start.19 = (f32[2,10,16,256]{3,2,1,0:T(8,128)S(1)}, f32[2,10,16,256]{3,2,1,0:T(8,128)}, u32[]{:S(2)}, u32[]{:S(2)}) collective-permute-start(f32[2,10,16,256]{3,2,1,0:T(8,128)S(1)} %slice_bitcast_fusion.4), channel_id=1, source_target_pairs={{0,192},{1,193},{2,194},{3,195},{4,196},{5,197},{6,198},{7,199},{8... | collective-permute-start | bytes 983048 | tf_op jit(solution)/shard_map/ppermute | solution.py:49
  113.4 15.2 %collective-permute-start.20 = (f32[2,10,16,256]{3,2,1,0:T(8,128)}, f32[2,10,16,256]{3,2,1,0:T(8,128)}, u32[]{:S(2)}, u32[]{:S(2)}) collective-permute-start(f32[2,10,16,256]{3,2,1,0:T(8,128)} %slice_bitcast_fusion.2), channel_id=1, source_target_pairs={{0,192},{1,193},{2,194},{3,195},{4,196},{5,197},{6,198},{7,199},{8... | collective-permute-start | bytes 983048 | tf_op jit(solution)/shard_map/ppermute | solution.py:49
  125.5 10.8 %collective-permute-start.10 = (f32[2,2,10,16,256]{4,3,2,1,0:T(8,128)}, f32[2,2,10,16,256]{4,3,2,1,0:T(8,128)S(1)}, u32[]{:S(2)}, u32[]{:S(2)}) collective-permute-start(f32[2,2,10,16,256]{4,3,2,1,0:T(8,128)} %get-tuple-element.69), channel_id=1, source_target_pairs={{0,64},{1,65},{2,66},{3,67},{4,68},{5,69},{6,70},{7,71},{8,72},{9,... | collective-permute-start | bytes 1966088 | tf_op jit(solution)/shard_map/ppermute | solution.py:49
  129.7 6.6 %copy-start.6 = (f32[2,2,10,16,256]{4,3,2,1,0:T(8,128)S(1)}, f32[2,2,10,16,256]{4,3,2,1,0:T(8,128)}, u32[]{:S(2)}) copy-start(f32[2,2,10,16,256]{4,3,2,1,0:T(8,128)} %get-tuple-element.66) | copy-start | bytes 1966084
  129.8 9.0 %collective-permute-start.22 = (f32[10,8,768]{2,1,0:T(8,128)S(1)}, f32[10,8,768]{2,1,0:T(8,128)S(1)}, u32[]{:S(2)}, u32[]{:S(2)}) collective-permute-start(f32[10,8,768]{2,1,0:T(8,128)S(1)} %get-tuple-element.92), channel_id=1, source_target_pairs={{0,1},{1,0},{2,3},{3,2},{4,5},{5,4},{6,7},{7,6},{8,9},{9,8},{10,11... | collective-permute-start | bytes 737288 | tf_op jit(solution)/shard_map/ppermute | solution.py:49
  132.1 9.9 %collective-permute-start.23 = (f32[10,8,768]{2,1,0:T(8,128)S(1)}, f32[10,8,768]{2,1,0:T(8,128)S(1)}, u32[]{:S(2)}, u32[]{:S(2)}) collective-permute-start(f32[10,8,768]{2,1,0:T(8,128)S(1)} %get-tuple-element.93), channel_id=1, source_target_pairs={{0,33},{1,32},{2,35},{3,34},{4,37},{5,36},{6,39},{7,38},{8,41},{9,... | collective-permute-start | bytes 737288 | tf_op jit(solution)/shard_map/ppermute | solution.py:49
  132.1 15.7 %collective-permute-start.21 = (f32[10,8,768]{2,1,0:T(8,128)S(1)}, f32[10,8,768]{2,1,0:T(8,128)S(1)}, u32[]{:S(2)}, u32[]{:S(2)}) collective-permute-start(f32[10,8,768]{2,1,0:T(8,128)S(1)} %slice.161), channel_id=1, source_target_pairs={{0,32},{1,33},{2,34},{3,35},{4,36},{5,37},{6,38},{7,39},{8,40},{9,... | collective-permute-start | bytes 737288 | tf_op jit(solution)/shard_map/ppermute | solution.py:49
  136.6 11.2 %collective-permute-start.11 = (f32[10,8,512]{2,1,0:T(8,128)S(1)}, f32[10,8,512]{2,1,0:T(8,128)S(1)}, u32[]{:S(2)}, u32[]{:S(2)}) collective-permute-start(f32[10,8,512]{2,1,0:T(8,128)S(1)} %get-tuple-element.94), channel_id=1, source_target_pairs={{0,192},{1,193},{2,194},{3,195},{4,196},{5,197},{6,198},{7,199},{8... | collective-permute-start | bytes 491528 | tf_op jit(solution)/shard_map/ppermute | solution.py:49
  137.2 10.7 %collective-permute-start.12 = (f32[10,8,512]{2,1,0:T(8,128)S(1)}, f32[10,8,512]{2,1,0:T(8,128)S(1)}, u32[]{:S(2)}, u32[]{:S(2)}) collective-permute-start(f32[10,8,512]{2,1,0:T(8,128)S(1)} %get-tuple-element.95), channel_id=1, source_target_pairs={{0,224},{1,225},{2,226},{3,227},{4,228},{5,229},{6,230},{7,231},{8... | collective-permute-start | bytes 491528 | tf_op jit(solution)/shard_map/ppermute | solution.py:49
  138.8 9.6 %collective-permute-start.13 = (f32[10,8,512]{2,1,0:T(8,128)S(1)}, f32[10,8,512]{2,1,0:T(8,128)S(1)}, u32[]{:S(2)}, u32[]{:S(2)}) collective-permute-start(f32[10,8,512]{2,1,0:T(8,128)S(1)} %get-tuple-element.96), channel_id=1, source_target_pairs={{0,193},{1,192},{2,195},{3,194},{4,197},{5,196},{6,199},{7,198},{8... | collective-permute-start | bytes 491528 | tf_op jit(solution)/shard_map/ppermute | solution.py:49
  141.9 8.7 %collective-permute-start.14 = (f32[10,8,512]{2,1,0:T(8,128)S(1)}, f32[10,8,512]{2,1,0:T(8,128)S(1)}, u32[]{:S(2)}, u32[]{:S(2)}) collective-permute-start(f32[10,8,512]{2,1,0:T(8,128)S(1)} %get-tuple-element.97), channel_id=1, source_target_pairs={{0,225},{1,224},{2,227},{3,226},{4,229},{5,228},{6,231},{7,230},{8... | collective-permute-start | bytes 491528 | tf_op jit(solution)/shard_map/ppermute | solution.py:49
  147.8 5.3 %collective-permute-start.15 = (f32[10,8,512]{2,1,0:T(8,128)S(1)}, f32[10,8,512]{2,1,0:T(8,128)S(1)}, u32[]{:S(2)}, u32[]{:S(2)}) collective-permute-start(f32[10,8,512]{2,1,0:T(8,128)S(1)} %get-tuple-element.98), channel_id=1, source_target_pairs={{0,1},{1,0},{2,3},{3,2},{4,5},{5,4},{6,7},{7,6},{8,9},{9,8},{10,11... | collective-permute-start | bytes 491528 | tf_op jit(solution)/shard_map/ppermute | solution.py:49
  147.8 6.3 %collective-permute-start.16 = (f32[10,8,512]{2,1,0:T(8,128)S(1)}, f32[10,8,512]{2,1,0:T(8,128)S(1)}, u32[]{:S(2)}, u32[]{:S(2)}) collective-permute-start(f32[10,8,512]{2,1,0:T(8,128)S(1)} %get-tuple-element.99), channel_id=1, source_target_pairs={{0,33},{1,32},{2,35},{3,34},{4,37},{5,36},{6,39},{7,38},{8,41},{9,... | collective-permute-start | bytes 491528 | tf_op jit(solution)/shard_map/ppermute | solution.py:49
  147.9 6.2 %collective-permute-start.17 = (f32[10,8,512]{2,1,0:T(8,128)S(1)}, f32[10,8,512]{2,1,0:T(8,128)S(1)}, u32[]{:S(2)}, u32[]{:S(2)}) collective-permute-start(f32[10,8,512]{2,1,0:T(8,128)S(1)} %slice.154), channel_id=1, source_target_pairs={{0,32},{1,33},{2,34},{3,35},{4,36},{5,37},{6,38},{7,39},{8,40},{9,... | collective-permute-start | bytes 491528 | tf_op jit(solution)/shard_map/ppermute | solution.py:49
  154.3 1.0 copy-start.8
Sparse Core Ops, SparseCore 0:
  9.1 49.1 all-gather.2
  60.1 38.7 all-gather.4
